TPU v7x, 768 devices: a whole 4x8x12 slice. The times are simulated.
768 devices in a mesh: fsdp: 12 (over z), tp: 64 (over x, y, core).
Axes of the slice: x: 4, y: 8, z: 12, core: 2. Of those that a mesh axis runs over, the one named last changes fastest.
Arguments:
- weight: float32 [6144, 32768], P('fsdp', 'tp'), may hold values from -6 to 6
- momentum: float32 [6144, 32768], P('fsdp', 'tp'), may hold values from -54 to 54
- gradient: bfloat16 [6144, 32768], P('fsdp', 'tp'), may hold values from -6 to 6
- right_basis: float32 [32768, 256], P('tp'), may hold values from -6 to 6
Outputs:
- new_weight: float32 [6144, 32768], P('fsdp', 'tp')
- new_momentum: float32 [6144, 32768], P('fsdp', 'tp')
- new_right: float32 [32768, 256], P('tp')
All inputs are finite; a program needn't handle non-finite values.
Results may differ from a plain program's by a relative error of at most 0.0003.
Values sent between devices are 32-bit elements; how exact they have to be, the bound alone decides.
No kernel may reach another device: no remote copies, remote signals or barrier semaphores. Data moves between devices by JAX's collectives and lax.ppermute only.
A program may use at most 32 MiB of HBM per device.

v0:
```python
import jax
import jax.numpy as jnp
from jax import lax
from jax.sharding import PartitionSpec as P

COLS = 32768


momentum_decay = 0.6
step_size = 2.0
epsilon_rms = 1e-06


def orthonormalize(rows_block, gram_matrix):
    factor = jnp.linalg.cholesky(gram_matrix)
    return jax.scipy.linalg.solve_triangular(factor, rows_block.T, lower=True).T


def body(weight, momentum, gradient, right_basis):
    highest = lax.Precision.HIGHEST
    buffer = momentum_decay * momentum + gradient.astype(jnp.float32)
    left_factor = lax.psum(jnp.dot(buffer, right_basis, precision=highest), "tp")
    gram_matrix = lax.psum(jnp.dot(left_factor.T, left_factor, precision=highest), "fsdp")
    orthonormal = orthonormalize(left_factor, gram_matrix)
    partial_right = jnp.dot(buffer.T, orthonormal, precision=highest)
    right_factor = lax.psum(partial_right, "fsdp")
    col_squares = lax.psum(jnp.sum(right_factor * right_factor, axis=0), "tp")
    col_scale = lax.rsqrt(col_squares / COLS + epsilon_rms)
    new_right = right_factor * col_scale[None, :]
    new_momentum = buffer - (1.0 - momentum_decay) * jnp.dot(
        orthonormal, right_factor.T, precision=highest
    )
    new_weight = weight - step_size * jnp.dot(orthonormal, new_right.T, precision=highest)
    return (new_weight, new_momentum, new_right)


def solution(mesh):
    placed = (P("fsdp", "tp"), P("fsdp", "tp"), P("fsdp", "tp"), P("tp", None))
    return jax.shard_map(
        body,
        mesh=mesh,
        in_specs=placed,
        out_specs=(P("fsdp", "tp"), P("fsdp", "tp"), P("tp", None)),
        check_vma=False,
    )
```

profile of v0, /device:TPU:1, one launch (start us, length us, event | category | flops | bytes accessed | tf_op | source)
XLA Modules:
  0.0 649.8 jit_solution(2062143724159203400)
XLA Ops:
  7.2 0.0 copy-start
  7.2 0.0 all-reduce.5.cloned.1.call-start
  7.2 1.0 copy-done
  8.2 3.2 fusion.3
  11.4 0.0 all-reduce.5.cloned.1.call-update
  11.5 0.0 all-reduce.7.cloned.1.call-start
  11.5 210.2 %all-reduce.5.cloned.1.call-done = f32[512,256]{1,0:T(8,128)} async-done(((f32[512,256]{1,0:T(8,128)}), f32[512,256]{1,0:T(8,128)}) %all-reduce.5.cloned.1.call-update) | async-done | bytes 524304 | tf_op jit(solution)/shard_map/psum | solution.py:22
  221.7 2.9 fusion.18
  224.6 0.0 all-reduce.7.cloned.1.call-update
  224.6 0.2 all-reduce.9.cloned.1.call-start
  224.9 103.5 %all-reduce.7.cloned.1.call-done = f32[256,256]{0,1:T(8,128)} async-done(((f32[256,256]{0,1:T(8,128)}), f32[256,256]{0,1:T(8,128)}) %all-reduce.7.cloned.1.call-update) | async-done | bytes 262160 | tf_op jit(solution)/shard_map/psum | solution.py:23
  328.4 0.0 copy-start.7
  328.4 1.1 copy.8
  329.6 0.0 copy-done.7
  329.7 11.7 %cholesky.50 = f32[128,128]{1,0:T(8,128)S(1)} custom-call(f32[128,128]{1,0:T(8,128)S(1)} %cholesky.118), custom_call_target="Cholesky" | custom-call | tf_op jit(solution)/shard_map/jit(cholesky)/cholesky | solution.py:15
  341.4 9.8 %custom-call.15 = f32[1,128,128]{1,2,0:T(8,128)S(1)} custom-call(f32[1,128,128]{2,1,0:T(8,128)S(1)} %get-tuple-element.24), custom_call_target="InvertDiagBlocksLowerTriangular" | custom-call | tf_op jit(solution)/shard_map/jit(cholesky)/cholesky | solution.py:15
  351.3 0.2 constant_dynamic-update-slice_fusion.1
  351.5 0.3 convolution_subtract_fusion.1
  351.7 11.7 %cholesky.105 = f32[128,128]{1,0:T(8,128)S(1)} custom-call(f32[128,128]{1,0:T(8,128)S(1)} %convolution_subtract_fusion.1), custom_call_target="Cholesky" | custom-call | tf_op jit(solution)/shard_map/jit(cholesky)/cholesky | solution.py:15
  363.5 0.6 compare_reduce_fusion
  365.4 0.0 copy-start.3
  365.5 0.1 triangular_solve.57
  365.5 4.2 while.1
  365.7 0.6 fusion.29
  366.3 1.4 bitcast_dynamic-update-slice_fusion.2
  367.7 0.6 fusion.29
  368.3 1.4 bitcast_dynamic-update-slice_fusion.2
  369.7 0.0 copy-start.1
  369.7 19.7 %custom-call.16 = f32[2,128,128]{1,2,0:T(8,128)S(1)} custom-call(f32[2,128,128]{2,1,0:T(8,128)S(1)} %get-tuple-element.10), custom_call_target="InvertDiagBlocksLowerTriangular" | custom-call | tf_op jit(solution)/shard_map/jit(_solve_triangular)/triangular_solve | solution.py:16
  389.4 0.0 copy-done.3
  389.4 0.4 fusion.4
  389.8 0.0 copy-start.2
  389.9 0.6 convolution_subtract_fusion
  390.5 0.4 fusion.8
  390.9 0.0 copy-done.1
  390.9 0.0 copy-done.2
  390.9 2.6 fusion.2
  393.5 0.0 all-reduce.9.cloned.1.call-update
  393.5 110.0 %all-reduce.9.cloned.1.call-done = f32[512,256]{1,0:T(8,128)} async-done(((f32[512,256]{1,0:T(8,128)}), f32[512,256]{1,0:T(8,128)}) %all-reduce.9.cloned.1.call-update) | async-done | bytes 524304 | tf_op jit(solution)/shard_map/psum | solution.py:26
  503.5 0.0 copy-start.4
  503.5 1.2 multiply_reduce_fusion
  504.7 131.7 %psum.31 = f32[256]{0:T(256)S(1)} all-reduce(f32[256]{0:T(256)S(1)} %multiply_reduce_fusion), channel_id=1, replica_groups=mesh['fsdp'=12,'tp'=64] {'tp'}, use_global_device_ids=true, to_apply=%region_8.9 | all-reduce | flops 256 | bytes 2048 | tf_op jit(solution)/shard_map/psum | solution.py:27
  636.4 0.0 copy-start.6
  636.4 0.0 copy-done.4
  636.4 1.2 copy-done.6
  637.6 0.0 copy-start.5
  637.6 2.8 fusion.1
  640.4 0.0 copy-done.5
  640.4 2.8 fusion
  (12 shorter events, 0.2 us)
Async XLA Ops:
  7.2 1.0 copy-start
  7.2 214.5 %all-reduce.5.cloned.1.call-start = ((), (), s32[]{:S(2)}) async-start(), calls=%async_computation | async-start | bytes 1048576 | tf_op jit(solution)/shard_map/psum | solution.py:22
  11.5 317.0 %all-reduce.7.cloned.1.call-start = ((), (), s32[]{:S(2)}) async-start(), calls=%async_computation.1 | async-start | bytes 524288 | tf_op jit(solution)/shard_map/psum | solution.py:23
  224.6 278.9 %all-reduce.9.cloned.1.call-start = ((), (), s32[]{:S(2)}) async-start(), calls=%async_computation.2 | async-start | bytes 1048576 | tf_op jit(solution)/shard_map/psum | solution.py:26
  328.4 1.2 copy-start.7
  365.4 24.0 %copy-start.3 = (f32[512,256]{1,0:T(8,128)S(1)}, f32[512,256]{1,0:T(8,128)}, u32[]{:S(2)}) copy-start(f32[512,256]{1,0:T(8,128)} %all-reduce.5.cloned.1.call-done) | copy-start | bytes 1572868
  369.7 21.2 %copy-start.1 = (f32[512,512]{1,0:T(8,128)S(1)}, f32[512,512]{1,0:T(8,128)}, u32[]{:S(2)}) copy-start(f32[512,512]{1,0:T(8,128)} %param.5) | copy-start | bytes 3145732
  389.8 1.0 copy-start.2
  503.5 132.9 %copy-start.4 = (f32[512,256]{1,0:T(8,128)S(1)}, f32[512,256]{1,0:T(8,128)}, u32[]{:S(2)}) copy-start(f32[512,256]{1,0:T(8,128)} %all-reduce.9.cloned.1.call-done) | copy-start | bytes 1572868
  636.4 1.2 copy-start.6
  637.6 2.8 copy-start.5
Sparse Core Ops, SparseCore 0:
  12.1 209.5 all-reduce.4
  224.8 103.6 all-reduce.6
  393.7 109.8 all-reduce.8
where the time goes:
time: 650 us
  waiting for transfers between devices  424 us (65%)
  blocking collectives  132 us (20%)
  other arithmetic  54.9 us (8%)
  matrix products  16.3 us (3%)
  between operations  15.2 us (2%)
  local copies, waits for them, and re-layouts  7.39 us (1%)
    psum x1, waiting for transfers between devices, body(): lax.psum(jnp.dot(buffer, right_basis, precision=highest), 'tp')  210 us
    psum x1, blocking collectives, body(): col_squares = lax.psum(jnp.sum(right_factor * right_factor, axis=0), 'tp')  132 us
    psum x1, waiting for transfers between devices, body(): right_factor = lax.psum(partial_right, 'fsdp')  110 us
    psum x1, waiting for transfers between devices, body(): lax.psum(jnp.dot(left_factor.T, left_factor, precision=highest), 'fsdp')  104 us
    another operation x6, other arithmetic, orthonormalize(): factor = jnp.linalg.cholesky(gram_matrix)  34 us
    another operation x3, other arithmetic, orthonormalize(): return jax.scipy.linalg.solve_triangular(factor, rows_block.T, lower=True).T  19.7 us
  transfers between devices with their start and end apart: 3, of which 3 were waited for; matrix products, arithmetic and copies ran while one was open for 0% of the time, Pallas kernels for 0%

commit v1 on v0

v1 whole, which is shorter than its diff:
```python
import jax
import jax.numpy as jnp
from jax import lax
from jax.sharding import Mesh, PartitionSpec as P

COLS = 32768

momentum_decay = 0.6
step_size = 2.0
epsilon_rms = 1e-06

PLANE = ("x", "y")
TP = ("x", "y", "core")


def exchange(blocks, axes):
    return lax.all_to_all(blocks, axes, 0, 0)


def spread(block, axes, size):
    return exchange(jnp.broadcast_to(block[None], (size,) + block.shape), axes)


def body(weight, momentum, gradient, right_basis):
    highest = lax.Precision.HIGHEST
    nz, nxy = lax.axis_size("z"), lax.axis_size("x") * lax.axis_size("y")
    rows, cols = momentum.shape
    rank = right_basis.shape[1]
    buffer = momentum_decay * momentum + gradient.astype(jnp.float32)
    partial = jnp.dot(buffer, right_basis, precision=highest)
    half = exchange(partial.reshape(2, rows // 2, rank), "core").sum(0)
    share = exchange(half.reshape(nxy, rows // (2 * nxy), rank), PLANE).sum(0)
    half = spread(share, PLANE, nxy).reshape(rows // 2, rank)
    left_factor = lax.all_gather(half, "core", axis=0, tiled=True)
    gram = jnp.dot(left_factor.T, left_factor, precision=highest)
    turned = jnp.dot(buffer.T, left_factor, precision=highest)
    both = jnp.concatenate([turned, gram], axis=0)
    piece = exchange(both.reshape(nz, (cols + rank) // nz, rank), "z").sum(0)
    both = lax.all_gather(piece, "z", axis=0, tiled=True)
    turned, gram = both[:cols], both[cols:]
    factor = jnp.linalg.cholesky(gram)
    inverse = jax.scipy.linalg.solve_triangular(
        factor, jnp.eye(rank, dtype=jnp.float32), lower=True
    )
    right_factor = jnp.dot(turned, inverse.T, precision=highest)
    orthonormal = jnp.dot(left_factor, inverse.T, precision=highest)
    squares = jnp.sum(right_factor * right_factor, axis=0, keepdims=True)
    col_squares = spread(squares, TP, 2 * nxy).sum(0)
    col_scale = lax.rsqrt(col_squares / COLS + epsilon_rms)
    new_right = right_factor * col_scale
    new_momentum = buffer - (1.0 - momentum_decay) * jnp.dot(
        orthonormal, right_factor.T, precision=highest
    )
    new_weight = weight - step_size * jnp.dot(orthonormal, new_right.T, precision=highest)
    return (new_weight, new_momentum, new_right)


def solution(mesh):
    fine = Mesh(mesh.devices.reshape(mesh.devices.shape[0], 4, -1, 2), ("z", "x", "y", "core"))
    placed = (P("z", TP), P("z", TP), P("z", TP), P(TP, None))
    return jax.shard_map(
        body,
        mesh=fine,
        in_specs=placed,
        out_specs=(P("z", TP), P("z", TP), P(TP, None)),
        check_vma=False,
    )
```

time: 650 us -> 219 us (0.34)
  waiting for transfers between devices: 424 us -> 34.6 us
  blocking collectives: 132 us -> 74.4 us
  starting transfers between devices: 0.3 us -> 22.8 us
  between operations: 15.2 us -> 2.16 us
    psum x3 -> x0, waiting for transfers between devices: 424 us -> none  [the longest x1 210 us: body(): lax.psum(jnp.dot(buffer, right_basis, precision=highest), 'tp')]
    psum x1 -> x0, blocking collectives: 132 us -> none  [body(): col_squares = lax.psum(jnp.sum(right_factor * right_factor, axis=0), 'tp')]
    all_to_all x0 -> x3, blocking collectives: none -> 43.4 us  [exchange(): return lax.all_to_all(blocks, axes, 0, 0)]
    all_to_all x0 -> x2, waiting for transfers between devices: none -> 34.6 us  [exchange(): return lax.all_to_all(blocks, axes, 0, 0)]
    all_gather x0 -> x2, blocking collectives: none -> 30.9 us  [the longest x1 25.4 us: body(): both = lax.all_gather(piece, 'z', axis=0, tiled=True)]
    all_to_all x0 -> x2, starting transfers between devices: none -> 22.8 us  [exchange(): return lax.all_to_all(blocks, axes, 0, 0)]
  transfers between devices with their start and end apart: 3 -> 2, of which waited for: 3 -> 2; matrix products, arithmetic and copies ran while one was open for 0% -> 1% of each run, Pallas kernels for 0% -> 0%
where the time goes in v1:
time: 219 us; the launch traced here: 218 us
  blocking collectives  74.4 us (34%)
  other arithmetic  56.7 us (26%)
  waiting for transfers between devices  34.6 us (16%)
  starting transfers between devices  22.8 us (10%)
  matrix products  16.2 us (7%)
  local copies, waits for them, and re-layouts  11.3 us (5%)
    all_to_all x3, blocking collectives, exchange(): return lax.all_to_all(blocks, axes, 0, 0)  43.4 us
    all_to_all x2, waiting for transfers between devices, exchange(): return lax.all_to_all(blocks, axes, 0, 0)  34.6 us
    another operation x6, other arithmetic, body(): factor = jnp.linalg.cholesky(gram)  33.9 us
    all_gather x1, blocking collectives, body(): both = lax.all_gather(piece, 'z', axis=0, tiled=True)  25.4 us
    all_to_all x2, starting transfers between devices, exchange(): return lax.all_to_all(blocks, axes, 0, 0)  22.8 us
    another operation x3, other arithmetic, body(): jax.scipy.linalg.solve_triangular(factor, jnp.eye(rank, dtype=jnp.float32...  20.5 us
    all_gather x1, blocking collectives, body(): left_factor = lax.all_gather(half, 'core', axis=0, tiled=True)  5.54 us
    another operation x6, local copies, waits for them, and re-layouts  5.19 us
  transfers between devices with their start and end apart: 2, of which 2 were waited for; matrix products, arithmetic and copies ran while one was open for 1% of the time, Pallas kernels for 0%

profile of v1, /device:TPU:1, one launch (start us, length us, event | category | flops | bytes accessed | tf_op | source)
XLA Modules:
  0.0 218.3 jit_solution(1894663594124247159)
XLA Ops:
  0.6 0.0 copy-start
  0.6 1.0 copy-done
  1.7 2.4 %fusion.5 = f32[512,256]{1,0:T(8,128)S(1)} fusion(f32[512,256]{1,0:T(8,128)S(1)} %copy-done, bf16[512,512]{1,0:T(8,128)(2,1)} %param.6, f32[512,512]{1,0:T(8,128)} %param.5), kind=kOutput, calls=%fused_computation.15 | convolution fusion | flops 806092800 | bytes 2621440 | tf_op jit(solution)/shard_map/dot_general | solution.py:30
  4.1 14.3 %all_to_all.25 = f32[2,256,256]{2,1,0:T(8,128)S(1)} all-to-all(f32[2,256,256]{2,1,0:T(8,128)S(1)} %bitcast.45), channel_id=1, replica_groups=mesh['z'=12,'x'=4,'y'=8,'core'=2] {'core'}, dimensions={0} | all-to-all | bytes 1048576 | tf_op jit(solution)/shard_map/all_to_all | solution.py:17
  18.4 13.2 %all_to_all.26 = f32[32,8,256]{2,1,0:T(8,128)S(1)} all-to-all(f32[32,8,256]{2,1,0:T(8,128)S(1)} %bitcast.47), channel_id=1, replica_groups=mesh['z'=12,'x'=4,'y'=8,'core'=2] {'x','y'}, dimensions={0} | all-to-all | bytes 524288 | tf_op jit(solution)/shard_map/all_to_all | solution.py:17
  31.7 16.0 %all_to_all.27 = f32[32,8,256]{2,1,0:T(8,128)S(1)} all-to-all(f32[32,8,256]{2,1,0:T(8,128)S(1)} %broadcast_in_dim.6), channel_id=1, replica_groups=mesh['z'=12,'x'=4,'y'=8,'core'=2] {'x','y'}, dimensions={0} | all-to-all | bytes 524288 | tf_op jit(solution)/shard_map/all_to_all | solution.py:17
  47.7 0.0 copy-start.1
  47.7 5.5 %all_gather.6 = f32[512,256]{1,0:T(8,128)S(1)} all-gather(f32[256,256]{1,0:T(8,128)S(1)} %bitcast.46), channel_id=1, replica_groups=mesh['z'=12,'x'=4,'y'=8,'core'=2] {'core'}, dimensions={0}, use_global_device_ids=true | all-gather | bytes 786432 | tf_op jit(solution)/shard_map/all_gather | solution.py:34
  53.2 0.0 copy-start.2
  53.2 1.0 fusion.20
  54.2 0.0 copy-done.1
  54.2 0.0 copy-done.2
  54.2 1.8 fusion.4
  56.1 0.9 pad_maximum_fusion
  57.0 12.0 %all-to-all-start.3 = ((f32[12,64,256]{2,1,0:T(8,128)}), f32[12,64,256]{2,1,0:T(8,128)S(1)}, u32[]{:S(2)}, u32[]{:S(2)}) async-start(f32[12,64,256]{2,1,0:T(8,128)} %bitcast.44), calls=%async_computation.3 | async-start | bytes 1572864 | tf_op jit(solution)/shard_map/all_to_all | solution.py:17
  69.1 28.0 %all-to-all-done.3 = f32[12,64,256]{2,1,0:T(8,128)S(1)} async-done(((f32[12,64,256]{2,1,0:T(8,128)}), f32[12,64,256]{2,1,0:T(8,128)S(1)}, u32[]{:S(2)}, u32[]{:S(2)}) %all-to-all-start.3) | async-done | bytes 786464 | tf_op jit(solution)/shard_map/all_to_all | solution.py:17
  97.0 0.1 reduce_sum.47
  97.1 25.4 %all_gather.7 = f32[768,256]{1,0:T(8,128)S(1)} all-gather(f32[64,256]{1,0:T(8,128)S(1)} %reduce_sum.47), channel_id=1, replica_groups=mesh['z'=12,'x'=4,'y'=8,'core'=2] {'z'}, dimensions={0}, use_global_device_ids=true | all-gather | bytes 851968 | tf_op jit(solution)/shard_map/all_gather | solution.py:39
  122.5 0.0 copy-start.4
  122.5 0.8 slice.67
  123.3 1.8 copy.16
  125.0 1.0 fusion.6
  126.0 0.0 copy-done.4
  126.0 0.0 copy-start.6
  126.1 0.7 copy-done.6
  126.8 0.0 copy-start.7
  126.8 11.7 %cholesky.50 = f32[128,128]{1,0:T(8,128)S(1)} custom-call(f32[128,128]{1,0:T(8,128)S(1)} %cholesky.118), custom_call_target="Cholesky" | custom-call | tf_op jit(solution)/shard_map/jit(cholesky)/cholesky | solution.py:41
  138.5 9.8 %custom-call.15 = f32[1,128,128]{1,2,0:T(8,128)S(1)} custom-call(f32[1,128,128]{2,1,0:T(8,128)S(1)} %get-tuple-element.24), custom_call_target="InvertDiagBlocksLowerTriangular" | custom-call | tf_op jit(solution)/shard_map/jit(cholesky)/cholesky | solution.py:41
  148.3 0.0 copy-done.7
  148.4 0.2 constant_dynamic-update-slice_fusion.1
  148.6 0.3 convolution_subtract_fusion.1
  148.8 11.7 %cholesky.105 = f32[128,128]{1,0:T(8,128)S(1)} custom-call(f32[128,128]{1,0:T(8,128)S(1)} %convolution_subtract_fusion.1), custom_call_target="Cholesky" | custom-call | tf_op jit(solution)/shard_map/jit(cholesky)/cholesky | solution.py:41
  160.6 0.6 compare_reduce_fusion
  162.6 0.1 triangular_solve.63
  162.6 5.4 %while.1 = (s32[]{:T(128)}, f32[256,256]{1,0:T(8,128)S(1)}, s32[2,2]{1,0:T(2,128)S(1)}, f32[2,128,128]{2,1,0:T(8,128)}, s32[]{:T(128)}) while((s32[]{:T(128)}, f32[256,256]{1,0:T(8,128)S(1)}, s32[2,2]{1,0:T(2,128)S(1)}, f32[2,128,128]{2,1,0:T(8,128)}, s32[]{:T(128)}) %tuple.28), condition=%wide.while_cond, body=%wide.while_body.sunk | while | flops 2 | bytes 132205 | solution.py:42
  162.8 0.6 fusion.35
  163.4 2.0 bitcast_dynamic-update-slice_fusion.2
  165.4 0.6 fusion.35
  166.0 2.0 bitcast_dynamic-update-slice_fusion.2
  168.0 20.5 %custom-call.16 = f32[2,128,128]{1,2,0:T(8,128)S(1)} custom-call(f32[2,128,128]{2,1,0:T(8,128)} %get-tuple-element.10), custom_call_target="InvertDiagBlocksLowerTriangular" | custom-call | tf_op jit(solution)/shard_map/jit(_solve_triangular)/triangular_solve | solution.py:42
  188.5 0.3 fusion.8
  188.8 0.3 convolution_subtract_fusion
  189.0 0.3 fusion.11
  189.4 1.7 multiply_reduce_fusion
  191.0 1.4 fusion.7
  192.5 0.7 broadcast_in_dim.7
  193.1 10.8 %all-to-all-start.4 = ((f32[64,1,256]{2,1,0:T(1,128)}), f32[64,1,256]{2,1,0:T(1,128)S(1)}, u32[]{:S(2)}, u32[]{:S(2)}) async-start(f32[64,1,256]{2,1,0:T(1,128)} %broadcast_in_dim.7), calls=%async_computation.4 | async-start | bytes 131072 | tf_op jit(solution)/shard_map/all_to_all | solution.py:17
  203.9 3.1 %fusion = f32[512,512]{1,0:T(8,128)} fusion(f32[512,256]{1,0:T(8,128)} %fusion.7, f32[512,256]{1,0:T(8,128)S(1)} %get-tuple-element.28, bf16[512,512]{1,0:T(8,128)(2,1)S(1)} %copy-done.2, f32[512,512]{1,0:T(8,128)S(1)} %copy-done.1), kind=kOutput, calls=%fused_computation.3 | convolution fusion | flops 806617088 | bytes 3670016 | tf_op jit(solution)/shard_map/dot_general | solution.py:51
  207.1 6.6 %all-to-all-done.4 = f32[64,1,256]{2,1,0:T(1,128)S(1)} async-done(((f32[64,1,256]{2,1,0:T(1,128)}), f32[64,1,256]{2,1,0:T(1,128)S(1)}, u32[]{:S(2)}, u32[]{:S(2)}) %all-to-all-start.4) | async-done | bytes 65568 | tf_op jit(solution)/shard_map/all_to_all | solution.py:17
  213.7 0.1 reduce_sum.49
  213.8 0.0 copy-start.3
  213.9 1.0 copy-done.3
  214.9 0.0 copy-start.5
  214.9 3.4 %fusion.1 = f32[512,512]{1,0:T(8,128)} fusion(f32[512,512]{1,0:T(8,128)} %param.4, f32[512,256]{1,0:T(8,128)S(1)} %copy-done.3, f32[512,256]{1,0:T(8,128)S(1)} %broadcast_multiply_fusion), kind=kOutput, calls=%fused_computation.5 | convolution fusion | flops 805830656 | bytes 3145728 | tf_op jit(solution)/shard_map/dot_general | solution.py:54
  218.3 0.0 copy-done.5
  (15 shorter events, 0.3 us)
Async XLA Ops:
  0.6 1.0 copy-start
  47.7 6.6 %copy-start.1 = (f32[512,512]{1,0:T(8,128)S(1)}, f32[512,512]{1,0:T(8,128)}, u32[]{:S(2)}) copy-start(f32[512,512]{1,0:T(8,128)} %param.5) | copy-start | bytes 3145732
  53.2 1.0 copy-start.2
  57.0 40.0 %all-to-all-start.3 = ((f32[12,64,256]{2,1,0:T(8,128)}), f32[12,64,256]{2,1,0:T(8,128)S(1)}, u32[]{:S(2)}, u32[]{:S(2)}) async-start(f32[12,64,256]{2,1,0:T(8,128)} %bitcast.44), calls=%async_computation.3 | async-start | bytes 1572864 | tf_op jit(solution)/shard_map/all_to_all | solution.py:17
  122.5 3.5 %copy-start.4 = (f32[768,256]{1,0:T(8,128)}, f32[768,256]{1,0:T(8,128)S(1)}, u32[]{:S(2)}) copy-start(f32[768,256]{1,0:T(8,128)S(1)} %all_gather.7) | copy-start | bytes 2359300
  126.0 0.7 copy-start.6
  126.8 21.6 %copy-start.7 = (f32[256,256]{1,0:T(8,128)S(1)}, f32[256,256]{1,0:T(8,128)}, u32[]{:S(2)}) copy-start(f32[256,256]{1,0:T(8,128)} %copy-done.6) | copy-start | bytes 786436
  193.1 20.6 %all-to-all-start.4 = ((f32[64,1,256]{2,1,0:T(1,128)}), f32[64,1,256]{2,1,0:T(1,128)S(1)}, u32[]{:S(2)}, u32[]{:S(2)}) async-start(f32[64,1,256]{2,1,0:T(1,128)} %broadcast_in_dim.7), calls=%async_computation.4 | async-start | bytes 131072 | tf_op jit(solution)/shard_map/all_to_all | solution.py:17
  213.8 1.0 copy-start.3
  214.9 3.4 %copy-start.5 = (f32[512,256]{1,0:T(8,128)}, f32[512,256]{1,0:T(8,128)S(1)}, u32[]{:S(2)}) copy-start(f32[512,256]{1,0:T(8,128)S(1)} %broadcast_multiply_fusion) | copy-start | bytes 1572868

commit v2 on v1

--- a/solution.py
+++ b/solution.py
@@ -1,6 +1,8 @@
 import jax
 import jax.numpy as jnp
 from jax import lax
+from jax.experimental import pallas as pl
+from jax.experimental.pallas import tpu as pltpu
 from jax.sharding import Mesh, PartitionSpec as P
 
 COLS = 32768
@@ -11,6 +13,114 @@
 
 PLANE = ("x", "y")
 TP = ("x", "y", "core")
+
+
+HIGHEST = lax.Precision.HIGHEST
+
+
+def mul(a, b):
+    return lax.dot_general(a, b, (((1,), (0,)), ((), ())), precision=HIGHEST, preferred_element_type=jnp.float32)
+
+
+def mul_tn(a, b):
+    return lax.dot_general(a, b, (((0,), (0,)), ((), ())), precision=HIGHEST, preferred_element_type=jnp.float32)
+
+
+def mul_nt(a, b):
+    return lax.dot_general(a, b, (((1,), (1,)), ((), ())), precision=HIGHEST, preferred_element_type=jnp.float32)
+
+
+def inverse_factor(tiles):
+    count = len(tiles)
+    shape = tiles[0].shape
+    lane = lax.broadcasted_iota(jnp.int32, shape, 1)
+    sub = lax.broadcasted_iota(jnp.int32, shape, 0)
+    out = []
+    for k in range(count):
+        first = 8 * k
+        own = (lane >= first) & (lane < first + 8)
+        top = tiles[k]
+        cols = [jnp.broadcast_to(top[:, first + s : first + s + 1], shape) for s in range(8)]
+        p = {
+            (t, s): jnp.broadcast_to(cols[s][t : t + 1, :], shape)
+            for s in range(8)
+            for t in range(s, 8)
+        }
+        unit = jnp.where(own, jnp.where(lane == first + sub, 1.0, 0.0), top)
+        row = [jnp.broadcast_to(unit[s : s + 1, :], shape) for s in range(8)]
+        low, inv = {}, []
+        for s in range(8):
+            inv.append(1.0 / p[s, s])
+            for t in range(s + 1, 8):
+                low[t, s] = p[t, s] * inv[s]
+            for t in range(s + 1, 8):
+                for u in range(s + 1, t + 1):
+                    p[t, u] = p[t, u] - low[t, s] * p[u, s]
+                row[t] = row[t] - low[t, s] * row[s]
+        done = row[0] * lax.rsqrt(p[0, 0])
+        for s in range(1, 8):
+            done = jnp.where(sub == s, row[s] * lax.rsqrt(p[s, s]), done)
+        out.append(jnp.where(lane < first + 8, done, 0.0))
+        if k + 1 == count:
+            break
+        back = [None] * 8
+        for s in range(7, -1, -1):
+            x = row[s] * inv[s]
+            for t in range(7, s, -1):
+                x = x - low[t, s] * back[t]
+            back[s] = x
+        for i in range(k + 1, count):
+            tile = tiles[i]
+            acc = jnp.where(own, 0.0, tile)
+            for s in range(8):
+                acc = acc - jnp.broadcast_to(tile[:, first + s : first + s + 1], shape) * back[s]
+            tiles[i] = acc
+    return out
+
+
+def factor_into(gram, inv_ref, block_ref):
+    n = block_ref.shape[1]
+
+    def run(at):
+        tiles = [block_ref[at, 8 * i : 8 * i + 8, :] for i in range(n // 8)]
+        for i, tile in enumerate(inverse_factor(tiles)):
+            block_ref[at, 8 * i : 8 * i + 8, :] = tile
+
+    block_ref[0] = gram[:n, :n]
+    block_ref[1] = gram[n:, n:]
+
+    def step(at, carry):
+        run(at)
+
+        @pl.when(at == 0)
+        def _():
+            one = block_ref[0]
+            cross = mul(one, gram[:n, n:])
+            block_ref[1] = block_ref[1] - mul_tn(cross, cross)
+            inv_ref[n:, :n] = mul_tn(cross, one)
+        return carry
+
+    lax.fori_loop(0, 2, step, 0)
+    inv_ref[:n, :n] = block_ref[0]
+    inv_ref[:n, n:] = jnp.zeros((n, n), jnp.float32)
+    inv_ref[n:, n:] = block_ref[1]
+    inv_ref[n:, :n] = -mul(block_ref[1], inv_ref[n:, :n])
+
+
+def chol_kernel(gram_ref, inv_ref, block_ref):
+    factor_into(gram_ref, inv_ref, block_ref)
+
+
+def inverse_cholesky(gram):
+    n = gram.shape[0]
+    return pl.pallas_call(
+        chol_kernel,
+        out_shape=jax.ShapeDtypeStruct((n, n), jnp.float32),
+        in_specs=[pl.BlockSpec(memory_space=pltpu.VMEM)],
+        out_specs=pl.BlockSpec(memory_space=pltpu.VMEM),
+        scratch_shapes=[pltpu.VMEM((2, n // 2, n // 2), jnp.float32)],
+        compiler_params=pltpu.CompilerParams(vmem_limit_bytes=32 * 1024 * 1024),
+    )(gram)
 
 
 def exchange(blocks, axes):
@@ -38,10 +148,7 @@
     piece = exchange(both.reshape(nz, (cols + rank) // nz, rank), "z").sum(0)
     both = lax.all_gather(piece, "z", axis=0, tiled=True)
     turned, gram = both[:cols], both[cols:]
-    factor = jnp.linalg.cholesky(gram)
-    inverse = jax.scipy.linalg.solve_triangular(
-        factor, jnp.eye(rank, dtype=jnp.float32), lower=True
-    )
+    inverse = inverse_cholesky(gram)
     right_factor = jnp.dot(turned, inverse.T, precision=highest)
     orthonormal = jnp.dot(left_factor, inverse.T, precision=highest)
     squares = jnp.sum(right_factor * right_factor, axis=0, keepdims=True)

time: 219 us -> 161 us (0.74)
  other arithmetic: 56.7 us -> 1.45 us
  blocking collectives: 74.4 us -> 115 us
  waiting for transfers between devices: 34.6 us -> 6.64 us
  starting transfers between devices: 22.8 us -> 10.7 us
  Pallas kernels: 0 us -> 9.71 us
  local copies, waits for them, and re-layouts: 11.3 us -> 2.74 us
  matrix products: 16.2 us -> 13.9 us
    another operation x9 -> x0, other arithmetic: 54.5 us -> none  [the longest x6 33.9 us: body(): factor = jnp.linalg.cholesky(gram)]
    all_to_all x3 -> x4, blocking collectives: 43.4 us -> 86.3 us  [exchange(): return lax.all_to_all(blocks, axes, 0, 0)]
    all_to_all x2 -> x1, waiting for transfers between devices: 34.6 us -> 6.64 us  [exchange(): return lax.all_to_all(blocks, axes, 0, 0)]
    all_to_all x2 -> x1, starting transfers between devices: 22.8 us -> 10.7 us  [exchange(): return lax.all_to_all(blocks, axes, 0, 0)]
    pallas_call x0 -> x1, Pallas kernels: none -> 9.71 us  [inverse_cholesky(): pl.pallas_call(chol_kernel, out_shape=jax.ShapeDtypeStruct((n, n), jnp.fl...]
    another operation x9 -> x0, local copies, waits for them, and re-layouts: 5.29 us -> none
    unnamed x17 -> x10, local copies, waits for them, and re-layouts: 4.53 us -> 2.04 us
    all_gather x1, blocking collectives: 25.4 us -> 22.9 us  [body(): both = lax.all_gather(piece, 'z', axis=0, tiled=True)]
  transfers between devices with their start and end apart: 2 -> 1, of which waited for: 2 -> 1; matrix products, arithmetic and copies ran while one was open for 1% -> 2% of each run, Pallas kernels for 0% -> 0%
where the time goes in v2:
time: 161 us
  blocking collectives  115 us (71%)
  matrix products  13.9 us (9%)
  starting transfers between devices  10.7 us (7%)
  Pallas kernels  9.71 us (6%)
  waiting for transfers between devices  6.64 us (4%)
  local copies, waits for them, and re-layouts  2.74 us (2%)
    all_to_all x4, blocking collectives, exchange(): return lax.all_to_all(blocks, axes, 0, 0)  86.3 us
    all_gather x1, blocking collectives, body(): both = lax.all_gather(piece, 'z', axis=0, tiled=True)  22.9 us
    all_to_all x1, starting transfers between devices, exchange(): return lax.all_to_all(blocks, axes, 0, 0)  10.7 us
    pallas_call x1, Pallas kernels, inverse_cholesky(): pl.pallas_call(chol_kernel, out_shape=jax.ShapeDtypeStruct((n, n), jnp.fl...  9.71 us
    all_to_all x1, waiting for transfers between devices, exchange(): return lax.all_to_all(blocks, axes, 0, 0)  6.64 us
    all_gather x1, blocking collectives, body(): left_factor = lax.all_gather(half, 'core', axis=0, tiled=True)  5.54 us
    dot_general x1, matrix products, body(): jnp.dot(orthonormal, new_right.T, precision=highest)  3.44 us
  transfers between devices with their start and end apart: 1, of which 1 were waited for; matrix products, arithmetic and copies ran while one was open for 2% of the time, Pallas kernels for 0%

profile of v2, /device:TPU:1, one launch (start us, length us, event | category | flops | bytes accessed | tf_op | source)
XLA Modules:
  0.0 160.6 jit_solution(13902777227342564609)
XLA Ops:
  0.6 0.0 copy-start
  0.6 1.0 copy-done
  1.7 2.4 %fusion.5 = f32[512,256]{1,0:T(8,128)S(1)} fusion(f32[512,256]{1,0:T(8,128)S(1)} %copy-done, bf16[512,512]{1,0:T(8,128)(2,1)} %param.6, f32[512,512]{1,0:T(8,128)} %param.5), kind=kOutput, calls=%fused_computation.10 | convolution fusion | flops 806092800 | bytes 2621440 | tf_op jit(solution)/shard_map/dot_general | solution.py:140
  4.1 14.3 %all_to_all.25 = f32[2,256,256]{2,1,0:T(8,128)S(1)} all-to-all(f32[2,256,256]{2,1,0:T(8,128)S(1)} %bitcast.16), channel_id=1, replica_groups=mesh['z'=12,'x'=4,'y'=8,'core'=2] {'core'}, dimensions={0} | all-to-all | bytes 1048576 | tf_op jit(solution)/shard_map/all_to_all | solution.py:127
  18.4 13.2 %all_to_all.26 = f32[32,8,256]{2,1,0:T(8,128)S(1)} all-to-all(f32[32,8,256]{2,1,0:T(8,128)S(1)} %bitcast.18), channel_id=1, replica_groups=mesh['z'=12,'x'=4,'y'=8,'core'=2] {'x','y'}, dimensions={0} | all-to-all | bytes 524288 | tf_op jit(solution)/shard_map/all_to_all | solution.py:127
  31.7 16.0 %all_to_all.27 = f32[32,8,256]{2,1,0:T(8,128)S(1)} all-to-all(f32[32,8,256]{2,1,0:T(8,128)S(1)} %broadcast_in_dim.4), channel_id=1, replica_groups=mesh['z'=12,'x'=4,'y'=8,'core'=2] {'x','y'}, dimensions={0} | all-to-all | bytes 524288 | tf_op jit(solution)/shard_map/all_to_all | solution.py:127
  47.7 0.0 copy-start.1
  47.7 5.5 %all_gather.6 = f32[512,256]{1,0:T(8,128)S(1)} all-gather(f32[256,256]{1,0:T(8,128)S(1)} %bitcast.17), channel_id=1, replica_groups=mesh['z'=12,'x'=4,'y'=8,'core'=2] {'core'}, dimensions={0}, use_global_device_ids=true | all-gather | bytes 786432 | tf_op jit(solution)/shard_map/all_gather | solution.py:144
  53.2 0.0 copy-start.2
  53.2 1.0 fusion.8
  54.2 0.0 copy-done.1
  54.2 0.0 copy-done.2
  54.2 1.8 %fusion.4 = f32[512,256]{1,0:T(8,128)S(1)} fusion(f32[512,256]{1,0:T(8,128)S(1)} %all_gather.6, bf16[512,512]{1,0:T(8,128)(2,1)S(1)} %copy-done.2, f32[512,512]{1,0:T(8,128)S(1)} %copy-done.1), kind=kOutput, calls=%fused_computation.9 | convolution fusion | flops 806092800 | bytes 2621440 | tf_op jit(solution)/shard_map/dot_general | solution.py:146
  56.1 0.1 pad_maximum_fusion
  56.1 42.8 %all_to_all.28 = f32[12,64,256]{2,1,0:T(8,128)} all-to-all(f32[12,64,256]{2,1,0:T(8,128)S(1)} %bitcast.15), channel_id=1, replica_groups=mesh['z'=12,'x'=4,'y'=8,'core'=2] {'z'}, dimensions={0} | all-to-all | bytes 1572864 | tf_op jit(solution)/shard_map/all_to_all | solution.py:127
  99.0 1.2 reduce_sum.47
  100.1 22.9 %all_gather.7 = f32[768,256]{1,0:T(8,128)S(1)} all-gather(f32[64,256]{1,0:T(8,128)S(1)} %reduce_sum.47), channel_id=1, replica_groups=mesh['z'=12,'x'=4,'y'=8,'core'=2] {'z'}, dimensions={0}, use_global_device_ids=true | all-gather | bytes 851968 | tf_op jit(solution)/shard_map/all_gather | solution.py:149
  123.1 9.7 %shard_map.67 = f32[256,256]{1,0:T(8,128)S(1)} custom-call(f32[256,256]{1,0:T(8,128)S(1)} %slice.8.gram_ref), custom_call_target="tpu_custom_call" | custom-call | tf_op jit(solution)/shard_map/pallas_call | solution.py:116
  132.8 0.6 multiply_reduce_fusion
  133.5 1.4 fusion.9
  134.9 0.7 broadcast_in_dim.5
  135.5 10.7 %all-to-all-start.4 = ((f32[64,1,256]{2,1,0:T(1,128)}), f32[64,1,256]{2,1,0:T(1,128)S(1)}, u32[]{:S(2)}, u32[]{:S(2)}) async-start(f32[64,1,256]{2,1,0:T(1,128)} %broadcast_in_dim.5), calls=%async_computation.4 | async-start | bytes 131072 | tf_op jit(solution)/shard_map/all_to_all | solution.py:127
  146.2 3.1 %fusion = f32[512,512]{1,0:T(8,128)} fusion(f32[512,256]{1,0:T(8,128)} %fusion.9, f32[512,256]{1,0:T(8,128)S(1)} %get-tuple-element.4, bf16[512,512]{1,0:T(8,128)(2,1)S(1)} %copy-done.2, f32[512,512]{1,0:T(8,128)S(1)} %copy-done.1), kind=kOutput, calls=%fused_computation.1 | convolution fusion | flops 806617088 | bytes 3670016 | tf_op jit(solution)/shard_map/dot_general | solution.py:158
  149.3 6.6 %all-to-all-done.4 = f32[64,1,256]{2,1,0:T(1,128)S(1)} async-done(((f32[64,1,256]{2,1,0:T(1,128)}), f32[64,1,256]{2,1,0:T(1,128)S(1)}, u32[]{:S(2)}, u32[]{:S(2)}) %all-to-all-start.4) | async-done | bytes 65568 | tf_op jit(solution)/shard_map/all_to_all | solution.py:127
  156.0 0.1 reduce_sum.49
  156.1 0.0 copy-start.3
  156.1 1.0 copy-done.3
  157.1 0.0 copy-start.4
  157.1 3.4 %fusion.1 = f32[512,512]{1,0:T(8,128)} fusion(f32[512,512]{1,0:T(8,128)} %param.4, f32[512,256]{1,0:T(8,128)S(1)} %copy-done.3, f32[512,256]{1,0:T(8,128)S(1)} %broadcast_multiply_fusion), kind=kOutput, calls=%fused_computation.3 | convolution fusion | flops 805830656 | bytes 3145728 | tf_op jit(solution)/shard_map/dot_general | solution.py:161
  160.6 0.0 copy-done.4
  (6 shorter events, 0.2 us)
Async XLA Ops:
  0.6 1.0 copy-start
  47.7 6.6 %copy-start.1 = (f32[512,512]{1,0:T(8,128)S(1)}, f32[512,512]{1,0:T(8,128)}, u32[]{:S(2)}) copy-start(f32[512,512]{1,0:T(8,128)} %param.5) | copy-start | bytes 3145732
  53.2 1.0 copy-start.2
  135.5 20.4 %all-to-all-start.4 = ((f32[64,1,256]{2,1,0:T(1,128)}), f32[64,1,256]{2,1,0:T(1,128)S(1)}, u32[]{:S(2)}, u32[]{:S(2)}) async-start(f32[64,1,256]{2,1,0:T(1,128)} %broadcast_in_dim.5), calls=%async_computation.4 | async-start | bytes 131072 | tf_op jit(solution)/shard_map/all_to_all | solution.py:127
  156.1 1.0 copy-start.3
  157.1 3.4 %copy-start.4 = (f32[512,256]{1,0:T(8,128)}, f32[512,256]{1,0:T(8,128)S(1)}, u32[]{:S(2)}) copy-start(f32[512,256]{1,0:T(8,128)S(1)} %broadcast_multiply_fusion) | copy-start | bytes 1572868

commit v3 on v2

--- a/solution.py
+++ b/solution.py
@@ -1,3 +1,4 @@
+import functools
 import jax
 import jax.numpy as jnp
 from jax import lax
@@ -13,7 +14,6 @@
 
 PLANE = ("x", "y")
 TP = ("x", "y", "core")
-
 
 HIGHEST = lax.Precision.HIGHEST
 
@@ -78,49 +78,137 @@
     return out
 
 
-def factor_into(gram, inv_ref, block_ref):
+def halves_of(x):
+    high = x.astype(jnp.bfloat16)
+    return high, (x - high.astype(jnp.float32)).astype(jnp.bfloat16)
+
+
+def right_kernel(top, both_ref, inv_ref, right_ref, sums_ref, block_ref, cross_ref, turned_ref):
     n = block_ref.shape[1]
-
-    def run(at):
+    nz, low = both_ref.shape[0], both_ref.shape[1] - top
+    cols = right_ref.shape[0]
+    parts = (block_ref.at[0], cross_ref, block_ref.at[1])
+    for at in range(nz):
+        for i in range(0, low, 8):
+            row = at * low + i
+            if row < 3 * n:
+                parts[row // n][row % n : row % n + 8, :] = both_ref[at, top + i : top + i + 8, :]
+        stop = min(2 * cols, (at + 1) * top)
+        if at * top < stop:
+            turned_ref[at * top : stop, :] = both_ref[at, : stop - at * top, :]
+
+    def step(at, carry):
         tiles = [block_ref[at, 8 * i : 8 * i + 8, :] for i in range(n // 8)]
         for i, tile in enumerate(inverse_factor(tiles)):
             block_ref[at, 8 * i : 8 * i + 8, :] = tile
 
-    block_ref[0] = gram[:n, :n]
-    block_ref[1] = gram[n:, n:]
-
-    def step(at, carry):
-        run(at)
-
         @pl.when(at == 0)
         def _():
-            one = block_ref[0]
-            cross = mul(one, gram[:n, n:])
+            first = block_ref[0]
+            cross = mul_nt(first, cross_ref[...])
             block_ref[1] = block_ref[1] - mul_tn(cross, cross)
-            inv_ref[n:, :n] = mul_tn(cross, one)
+            cross_ref[...] = mul_tn(cross, first)
+
         return carry
 
     lax.fori_loop(0, 2, step, 0)
-    inv_ref[:n, :n] = block_ref[0]
+    first, last = block_ref[0], block_ref[1]
+    cross = -mul(last, cross_ref[...])
+    inv_ref[:n, :n] = first
     inv_ref[:n, n:] = jnp.zeros((n, n), jnp.float32)
-    inv_ref[n:, n:] = block_ref[1]
-    inv_ref[n:, :n] = -mul(block_ref[1], inv_ref[n:, :n])
-
-
-def chol_kernel(gram_ref, inv_ref, block_ref):
-    factor_into(gram_ref, inv_ref, block_ref)
-
-
-def inverse_cholesky(gram):
-    n = gram.shape[0]
+    inv_ref[n:, :n] = cross
+    inv_ref[n:, n:] = last
+    left, right = turned_ref[:cols, :], turned_ref[cols:, :]
+    left, right = mul_nt(left, first), mul_nt(left, cross) + mul_nt(right, last)
+    right_ref[:, :n] = left
+    right_ref[:, n:] = right
+    left = jnp.sum(left * left, axis=0, keepdims=True)
+    right = jnp.sum(right * right, axis=0, keepdims=True)
+    sums_ref[:, :, :n] = jnp.broadcast_to(left[None], (sums_ref.shape[0], 1, n))
+    sums_ref[:, :, n:] = jnp.broadcast_to(right[None], (sums_ref.shape[0], 1, n))
+
+
+def whole(kernel, shapes, scratch=(), limit=32, cost=(10**9, 2**22), **kw):
     return pl.pallas_call(
-        chol_kernel,
-        out_shape=jax.ShapeDtypeStruct((n, n), jnp.float32),
-        in_specs=[pl.BlockSpec(memory_space=pltpu.VMEM)],
-        out_specs=pl.BlockSpec(memory_space=pltpu.VMEM),
-        scratch_shapes=[pltpu.VMEM((2, n // 2, n // 2), jnp.float32)],
-        compiler_params=pltpu.CompilerParams(vmem_limit_bytes=32 * 1024 * 1024),
-    )(gram)
+        kernel,
+        out_shape=shapes,
+        scratch_shapes=list(scratch),
+        compiler_params=pltpu.CompilerParams(vmem_limit_bytes=limit * 1024 * 1024),
+        cost_estimate=pl.CostEstimate(flops=cost[0], bytes_accessed=cost[1], transcendentals=0),
+        **kw,
+    )
+
+
+def f32(*shape):
+    return jax.ShapeDtypeStruct(shape, jnp.float32)
+
+
+def turn_kernel(top, momentum_ref, gradient_ref, left_ref, out_ref):
+    nz, both, n = out_ref.shape
+    low = both - top
+    cols = momentum_ref.shape[1]
+    left = left_ref[...]
+    square = mul_tn(left, left)
+    blocks = (square[:n, :n], square[n:, :n], square[n:, n:])
+    buffer = momentum_decay * momentum_ref[...] + gradient_ref[...].astype(jnp.float32)
+    turned = mul_tn(buffer, left)
+    for at in range(nz):
+        for start, side in ((0, 0), (cols, 1)):
+            lo, hi = max(at * top, start), min((at + 1) * top, start + cols)
+            if lo < hi:
+                out_ref[at, lo - at * top : hi - at * top, :] = turned[lo - start : hi - start, side * n : side * n + n]
+        fill = max(2 * cols - at * top, 0)
+        if fill < top:
+            out_ref[at, fill:top, :] = jnp.zeros((top - fill, n), jnp.float32)
+        for i in range(0, low, 8):
+            row = at * low + i
+            if row < 3 * n:
+                out_ref[at, top + i : top + i + 8, :] = blocks[row // n][row % n : row % n + 8, :]
+            else:
+                out_ref[at, top + i : top + i + 8, :] = jnp.zeros((8, n), jnp.float32)
+
+
+def products(a, b):
+    head, tail = halves_of(a)
+    high, low = halves_of(b)
+    part = functools.partial(lax.dot_general, dimension_numbers=(((1,), (1,)), ((), ())), preferred_element_type=jnp.float32)
+    return part(head, high) + (part(head, low) + part(tail, high))
+
+
+def momentum_kernel(inv_ref, left_ref, right_ref, momentum_ref, gradient_ref, new_momentum_ref, basis_ref):
+    basis = mul_nt(left_ref[...], inv_ref[...])
+    basis_ref[...] = basis
+    buffer = momentum_decay * momentum_ref[...] + gradient_ref[...].astype(jnp.float32)
+    new_momentum_ref[...] = buffer - (1.0 - momentum_decay) * products(basis, right_ref[...])
+
+
+def weight_kernel(sums_ref, weight_ref, basis_ref, right_ref, new_weight_ref, new_right_ref):
+    scale = lax.rsqrt(jnp.sum(sums_ref[...], axis=0) / COLS + epsilon_rms)
+
+    @pl.when(pl.program_id(0) == 0)
+    def _():
+        new_right_ref[...] = right_ref[...] * scale
+
+    new_weight_ref[...] = weight_ref[...] - step_size * products(basis_ref[...], new_right_ref[...])
+
+
+def weight_step(sums, weight, basis, right):
+    rows, cols = weight.shape
+    rank = right.shape[1]
+    block = rows // 4
+    whole_spec = pl.BlockSpec((cols, rank), lambda i: (0, 0))
+    return whole(
+        weight_kernel,
+        (f32(rows, cols), f32(cols, rank)),
+        grid=(rows // block,),
+        in_specs=[
+            pl.BlockSpec(sums.shape, lambda i: (0, 0, 0)),
+            pl.BlockSpec((block, cols), lambda i: (i, 0)),
+            pl.BlockSpec((block, rank), lambda i: (i, 0)),
+            whole_spec,
+        ],
+        out_specs=(pl.BlockSpec((block, cols), lambda i: (i, 0)), whole_spec),
+    )(sums, weight, basis, right)
 
 
 def exchange(blocks, axes):
@@ -142,23 +230,26 @@
     share = exchange(half.reshape(nxy, rows // (2 * nxy), rank), PLANE).sum(0)
     half = spread(share, PLANE, nxy).reshape(rows // 2, rank)
     left_factor = lax.all_gather(half, "core", axis=0, tiled=True)
-    gram = jnp.dot(left_factor.T, left_factor, precision=highest)
-    turned = jnp.dot(buffer.T, left_factor, precision=highest)
-    both = jnp.concatenate([turned, gram], axis=0)
-    piece = exchange(both.reshape(nz, (cols + rank) // nz, rank), "z").sum(0)
-    both = lax.all_gather(piece, "z", axis=0, tiled=True)
-    turned, gram = both[:cols], both[cols:]
-    inverse = inverse_cholesky(gram)
-    right_factor = jnp.dot(turned, inverse.T, precision=highest)
-    orthonormal = jnp.dot(left_factor, inverse.T, precision=highest)
-    squares = jnp.sum(right_factor * right_factor, axis=0, keepdims=True)
-    col_squares = spread(squares, TP, 2 * nxy).sum(0)
-    col_scale = lax.rsqrt(col_squares / COLS + epsilon_rms)
-    new_right = right_factor * col_scale
-    new_momentum = buffer - (1.0 - momentum_decay) * jnp.dot(
-        orthonormal, right_factor.T, precision=highest
+    half = rank // 2
+    top = -(-2 * cols // (8 * nz)) * 8
+    low = -(-3 * half // (8 * nz)) * 8
+    pieces = whole(functools.partial(turn_kernel, top), f32(nz, top + low, half))(
+        momentum, gradient, left_factor
     )
-    new_weight = weight - step_size * jnp.dot(orthonormal, new_right.T, precision=highest)
+    piece = exchange(pieces, "z").sum(0)
+    both = lax.all_gather(piece, "z")
+    scratch = [(2, half, half), (half, half), (2 * cols, half)]
+    inverse, right_factor, sums = whole(
+        functools.partial(right_kernel, top),
+        (f32(rank, rank), f32(cols, rank), f32(2 * nxy, 1, rank)),
+        [pltpu.VMEM(shape, jnp.float32) for shape in scratch],
+        cost=(10**10, 2**25),
+    )(both)
+    sums = exchange(sums, TP)
+    new_momentum, orthonormal = whole(
+        momentum_kernel, (f32(rows, cols), f32(rows, rank)), cost=(10**9, 2**24)
+    )(inverse, left_factor, right_factor, momentum, gradient)
+    new_weight, new_right = weight_step(sums, weight, orthonormal, right_factor)
     return (new_weight, new_momentum, new_right)
 
 

time: 161 us -> 156 us (0.969)
  matrix products: 13.9 us -> 2.43 us
  Pallas kernels: 9.71 us -> 18.5 us
  blocking collectives: 115 us -> 113 us
    dot_general x6 -> x0, matrix products: 11.5 us -> none  [the longest x1 3.44 us: body(): jnp.dot(orthonormal, new_right.T, precision=highest)]
    pallas_call x1 -> x4, Pallas kernels: 9.71 us -> 18.5 us  [the longest x1 11.3 us: body(): whole(functools.partial(right_kernel, top), (f32(rank, rank), f32(cols, r...]
    unnamed x10 -> x12, local copies, waits for them, and re-layouts: 2.04 us -> 4.11 us
  transfers between devices with their start and end apart: 1 -> 1, of which waited for: 1 -> 1; matrix products, arithmetic and copies ran while one was open for 2% -> 0% of each run, Pallas kernels for 0% -> 2%
where the time goes in v3:
time: 156 us
  blocking collectives  113 us (72%)
  Pallas kernels  18.5 us (12%)
  starting transfers between devices  10.5 us (7%)
  waiting for transfers between devices  6.22 us (4%)
  local copies, waits for them, and re-layouts  4.12 us (3%)
  matrix products  2.43 us (2%)
    all_to_all x4, blocking collectives, exchange(): return lax.all_to_all(blocks, axes, 0, 0)  84.8 us
    all_gather x1, blocking collectives, body(): both = lax.all_gather(piece, 'z')  22.6 us
    pallas_call x1, Pallas kernels, body(): whole(functools.partial(right_kernel, top), (f32(rank, rank), f32(cols, r...  11.3 us
    all_to_all x1, starting transfers between devices, exchange(): return lax.all_to_all(blocks, axes, 0, 0)  10.5 us
    all_to_all x1, waiting for transfers between devices, exchange(): return lax.all_to_all(blocks, axes, 0, 0)  6.22 us
    all_gather x1, blocking collectives, body(): left_factor = lax.all_gather(half, 'core', axis=0, tiled=True)  5.54 us
    unnamed x12, local copies, waits for them, and re-layouts  4.11 us
  transfers between devices with their start and end apart: 1, of which 1 were waited for; matrix products, arithmetic and copies ran while one was open for 0% of the time, Pallas kernels for 2%

profile of v3, /device:TPU:1, one launch (start us, length us, event | category | flops | bytes accessed | tf_op | source)
XLA Modules:
  0.0 155.5 jit_solution(17044523407248753090)
XLA Ops:
  0.6 0.0 copy-start
  0.6 1.0 copy-done
  1.7 2.4 %fusion = f32[512,256]{1,0:T(8,128)S(1)} fusion(f32[512,256]{1,0:T(8,128)S(1)} %copy-done, bf16[512,512]{1,0:T(8,128)(2,1)} %gradient_ref.3, f32[512,512]{1,0:T(8,128)} %momentum_ref.3), kind=kOutput, calls=%fused_computation | convolution fusion | flops 806092800 | bytes 2621440 | tf_op jit(solution)/shard_map/dot_general | solution.py:228
  4.1 14.3 %all_to_all.25 = f32[2,256,256]{2,1,0:T(8,128)S(1)} all-to-all(f32[2,256,256]{2,1,0:T(8,128)S(1)} %bitcast.6), channel_id=1, replica_groups=mesh['z'=12,'x'=4,'y'=8,'core'=2] {'core'}, dimensions={0} | all-to-all | bytes 1048576 | tf_op jit(solution)/shard_map/all_to_all | solution.py:215
  18.4 13.2 %all_to_all.26 = f32[32,8,256]{2,1,0:T(8,128)S(1)} all-to-all(f32[32,8,256]{2,1,0:T(8,128)S(1)} %bitcast.8), channel_id=1, replica_groups=mesh['z'=12,'x'=4,'y'=8,'core'=2] {'x','y'}, dimensions={0} | all-to-all | bytes 524288 | tf_op jit(solution)/shard_map/all_to_all | solution.py:215
  31.6 0.0 copy-start.1
  31.7 16.1 %all_to_all.27 = f32[32,8,256]{2,1,0:T(8,128)S(1)} all-to-all(f32[32,8,256]{2,1,0:T(8,128)S(1)} %broadcast_in_dim.2), channel_id=1, replica_groups=mesh['z'=12,'x'=4,'y'=8,'core'=2] {'x','y'}, dimensions={0} | all-to-all | bytes 524288 | tf_op jit(solution)/shard_map/all_to_all | solution.py:215
  47.8 0.0 copy-start.2
  47.8 5.5 %all_gather.9.left_ref = f32[512,256]{1,0:T(8,128)S(1)} all-gather(f32[256,256]{1,0:T(8,128)S(1)} %bitcast.7), channel_id=1, replica_groups=mesh['z'=12,'x'=4,'y'=8,'core'=2] {'core'}, dimensions={0}, use_global_device_ids=true | all-gather | bytes 786432 | tf_op jit(solution)/shard_map/all_gather | solution.py:232
  53.3 0.0 copy-done.1
  53.3 0.0 copy-done.2
  53.3 1.5 shard_map.67
  54.9 41.3 %all_to_all.28 = f32[12,120,128]{2,1,0:T(8,128)S(1)} all-to-all(f32[12,120,128]{2,1,0:T(8,128)S(1)} %shard_map.67), channel_id=1, replica_groups=mesh['z'=12,'x'=4,'y'=8,'core'=2] {'z'}, dimensions={0} | all-to-all | bytes 1474560 | tf_op jit(solution)/shard_map/all_to_all | solution.py:215
  96.2 22.6 %all-gather = f32[1440,128]{1,0:T(8,128)S(1)} all-gather(f32[120,128]{1,0:T(8,128)S(1)} %reduce_sum.29), channel_id=2, replica_groups=mesh['z'=12,'x'=4,'y'=8,'core'=2] {'z'}, dimensions={0}, use_global_device_ids=true | all-gather | bytes 798720 | tf_op jit(solution)/shard_map/all_gather | solution.py:240
  118.8 11.3 %shard_map.68 = (f32[256,256]{1,0:T(8,128)S(1)}, f32[512,256]{1,0:T(8,128)S(1)}, f32[64,1,256]{2,1,0:T(1,128)}) custom-call(f32[12,120,128]{2,1,0:T(8,128)S(1)} %bitcast.5), custom_call_target="tpu_custom_call" | custom-call | flops 10000000000 | bytes 33554432 | tf_op jit(solution)/shard_map/pallas_call | solution.py:242
  130.1 10.5 %all-to-all-start.4 = ((f32[64,1,256]{2,1,0:T(1,128)}), f32[64,1,256]{2,1,0:T(1,128)S(1)}, u32[]{:S(2)}, u32[]{:S(2)}) async-start(f32[64,1,256]{2,1,0:T(1,128)} %get-tuple-element.10), calls=%async_computation.4 | async-start | bytes 131072 | tf_op jit(solution)/shard_map/all_to_all | solution.py:215
  140.6 2.8 %shard_map.69 = (f32[512,512]{1,0:T(8,128)}, f32[512,256]{1,0:T(8,128)S(1)}) custom-call(f32[256,256]{1,0:T(8,128)S(1)} %get-tuple-element.11.inv_ref, f32[512,256]{1,0:T(8,128)S(1)} %all_gather.9.left_ref, f32[512,256]{1,0:T(8,128)S(1)} %get-tuple-element.12.right_ref, f32[512,512]{1,0:T(8,128)S(1)} %copy-done.1, bf16[512,512]{1,0:T(8,128)(2,1)S(1)} %copy-done.2), custom_call_target="tpu_custom_call" | custom-call | flops 1000000000 | bytes 16777216 | tf_op jit(solution)/shard_map/pallas_call | solution.py:249
  143.4 0.0 copy-start.4
  143.4 0.8 copy-done.4
  144.1 6.2 %all-to-all-done.4.sums_ref = f32[64,1,256]{2,1,0:T(1,128)S(1)} async-done(((f32[64,1,256]{2,1,0:T(1,128)}), f32[64,1,256]{2,1,0:T(1,128)S(1)}, u32[]{:S(2)}, u32[]{:S(2)}) %all-to-all-start.4) | async-done | bytes 65568 | tf_op jit(solution)/shard_map/all_to_all | solution.py:215
  150.4 0.0 copy-start.3
  150.4 1.2 copy-done.3
  151.6 0.0 copy-start.5
  151.6 1.0 copy-done.5
  152.6 2.9 %shard_map.70 = (f32[512,512]{1,0:T(8,128)}, f32[512,256]{1,0:T(8,128)}) custom-call(f32[64,1,256]{2,1,0:T(1,128)S(1)} %all-to-all-done.4.sums_ref, f32[512,512]{1,0:T(8,128)S(1)} %copy-done.3, f32[512,256]{1,0:T(8,128)S(1)} %copy-done.5, f32[512,256]{1,0:T(8,128)S(1)} %get-tuple-element.12.right_ref), custom_call_target="tpu_custom_call" | custom-call | flops 1000000000 | bytes 4194304 | tf_op jit(solution)/shard_map/pallas_call | solution.py:200
  (4 shorter events, 0.1 us)
Async XLA Ops:
  0.6 1.0 copy-start
  31.6 21.7 %copy-start.1 = (f32[512,512]{1,0:T(8,128)S(1)}, f32[512,512]{1,0:T(8,128)}, u32[]{:S(2)}) copy-start(f32[512,512]{1,0:T(8,128)} %momentum_ref.3) | copy-start | bytes 3145732
  47.8 5.5 %copy-start.2 = (bf16[512,512]{1,0:T(8,128)(2,1)S(1)}, bf16[512,512]{1,0:T(8,128)(2,1)}, u32[]{:S(2)}) copy-start(bf16[512,512]{1,0:T(8,128)(2,1)} %gradient_ref.3) | copy-start | bytes 1572868
  130.1 20.3 %all-to-all-start.4 = ((f32[64,1,256]{2,1,0:T(1,128)}), f32[64,1,256]{2,1,0:T(1,128)S(1)}, u32[]{:S(2)}, u32[]{:S(2)}) async-start(f32[64,1,256]{2,1,0:T(1,128)} %get-tuple-element.10), calls=%async_computation.4 | async-start | bytes 131072 | tf_op jit(solution)/shard_map/all_to_all | solution.py:215
  143.4 0.8 copy-start.4
  150.4 1.2 copy-start.3
  151.6 1.0 copy-start.5

commit v4 on v3

--- a/solution.py
+++ b/solution.py
@@ -30,7 +30,7 @@
     return lax.dot_general(a, b, (((1,), (1,)), ((), ())), precision=HIGHEST, preferred_element_type=jnp.float32)
 
 
-def inverse_factor(tiles):
+def inverse_factor(tiles, wide_ref):
     count = len(tiles)
     shape = tiles[0].shape
     lane = lax.broadcasted_iota(jnp.int32, shape, 1)
@@ -41,13 +41,12 @@
         own = (lane >= first) & (lane < first + 8)
         top = tiles[k]
         cols = [jnp.broadcast_to(top[:, first + s : first + s + 1], shape) for s in range(8)]
-        p = {
-            (t, s): jnp.broadcast_to(cols[s][t : t + 1, :], shape)
-            for s in range(8)
-            for t in range(s, 8)
-        }
+        for s in range(8):
+            wide_ref[k % 2, 8 * s : 8 * s + 8, :] = cols[s]
         unit = jnp.where(own, jnp.where(lane == first + sub, 1.0, 0.0), top)
-        row = [jnp.broadcast_to(unit[s : s + 1, :], shape) for s in range(8)]
+        wide_ref[k % 2, 64:, :] = unit
+        p = {(t, s): wide_ref[k % 2, pl.ds(8 * s + t, 8, stride=0), :] for s in range(8) for t in range(s, 8)}
+        row = [wide_ref[k % 2, pl.ds(64 + s, 8, stride=0), :] for s in range(8)]
         low, inv = {}, []
         for s in range(8):
             inv.append(1.0 / p[s, s])
@@ -72,7 +71,7 @@
         for i in range(k + 1, count):
             tile = tiles[i]
             acc = jnp.where(own, 0.0, tile)
-            for s in range(8):
+            for s in range(7, -1, -1):
                 acc = acc - jnp.broadcast_to(tile[:, first + s : first + s + 1], shape) * back[s]
             tiles[i] = acc
     return out
@@ -83,7 +82,7 @@
     return high, (x - high.astype(jnp.float32)).astype(jnp.bfloat16)
 
 
-def right_kernel(top, both_ref, inv_ref, right_ref, sums_ref, block_ref, cross_ref, turned_ref):
+def right_kernel(top, both_ref, inv_ref, right_ref, sums_ref, block_ref, cross_ref, turned_ref, wide_ref):
     n = block_ref.shape[1]
     nz, low = both_ref.shape[0], both_ref.shape[1] - top
     cols = right_ref.shape[0]
@@ -99,7 +98,7 @@
 
     def step(at, carry):
         tiles = [block_ref[at, 8 * i : 8 * i + 8, :] for i in range(n // 8)]
-        for i, tile in enumerate(inverse_factor(tiles)):
+        for i, tile in enumerate(inverse_factor(tiles, wide_ref)):
             block_ref[at, 8 * i : 8 * i + 8, :] = tile
 
         @pl.when(at == 0)
@@ -168,9 +167,9 @@
                 out_ref[at, top + i : top + i + 8, :] = jnp.zeros((8, n), jnp.float32)
 
 
-def products(a, b):
+def products(a, halves):
     head, tail = halves_of(a)
-    high, low = halves_of(b)
+    high, low = halves
     part = functools.partial(lax.dot_general, dimension_numbers=(((1,), (1,)), ((), ())), preferred_element_type=jnp.float32)
     return part(head, high) + (part(head, low) + part(tail, high))
 
@@ -179,35 +178,49 @@
     basis = mul_nt(left_ref[...], inv_ref[...])
     basis_ref[...] = basis
     buffer = momentum_decay * momentum_ref[...] + gradient_ref[...].astype(jnp.float32)
-    new_momentum_ref[...] = buffer - (1.0 - momentum_decay) * products(basis, right_ref[...])
-
-
-def weight_kernel(sums_ref, weight_ref, basis_ref, right_ref, new_weight_ref, new_right_ref):
+    new_momentum_ref[...] = buffer - (1.0 - momentum_decay) * products(basis, halves_of(right_ref[...]))
+
+
+def weight_kernel(sums_ref, weight_ref, basis_ref, right_ref, new_weight_ref, new_right_ref, block_ref, scaled_ref, in_sems, out_sems):
+    count, size = block_ref.shape[:2]
+    rows = [pl.ds(i * size, size) for i in range(count)]
+    loads = [pltpu.make_async_copy(weight_ref.at[rows[i]], block_ref.at[i], in_sems.at[i]) for i in range(count)]
+    stores = [pltpu.make_async_copy(block_ref.at[i], new_weight_ref.at[rows[i]], out_sems.at[i]) for i in range(count)]
+    for load in loads:
+        load.start()
     scale = lax.rsqrt(jnp.sum(sums_ref[...], axis=0) / COLS + epsilon_rms)
-
-    @pl.when(pl.program_id(0) == 0)
-    def _():
-        new_right_ref[...] = right_ref[...] * scale
-
-    new_weight_ref[...] = weight_ref[...] - step_size * products(basis_ref[...], new_right_ref[...])
+    new_right = right_ref[...] * scale
+    scaled_ref[...] = new_right
+    last = pltpu.make_async_copy(scaled_ref, new_right_ref, out_sems.at[count])
+    last.start()
+    scaled = halves_of(new_right)
+    for i in range(count):
+        product = products(basis_ref[rows[i], :], scaled)
+        loads[i].wait()
+        block_ref[i] = block_ref[i] - step_size * product
+        stores[i].start()
+    for store in stores:
+        store.wait()
+    last.wait()
 
 
 def weight_step(sums, weight, basis, right):
     rows, cols = weight.shape
     rank = right.shape[1]
-    block = rows // 4
-    whole_spec = pl.BlockSpec((cols, rank), lambda i: (0, 0))
+    count = 2
+    vmem, anywhere = pl.BlockSpec(memory_space=pltpu.VMEM), pl.BlockSpec(memory_space=pl.ANY)
     return whole(
         weight_kernel,
         (f32(rows, cols), f32(cols, rank)),
-        grid=(rows // block,),
-        in_specs=[
-            pl.BlockSpec(sums.shape, lambda i: (0, 0, 0)),
-            pl.BlockSpec((block, cols), lambda i: (i, 0)),
-            pl.BlockSpec((block, rank), lambda i: (i, 0)),
-            whole_spec,
+        [
+            pltpu.VMEM((count, rows // count, cols), jnp.float32),
+            pltpu.VMEM((cols, rank), jnp.float32),
+            pltpu.SemaphoreType.DMA((count,)),
+            pltpu.SemaphoreType.DMA((count + 1,)),
         ],
-        out_specs=(pl.BlockSpec((block, cols), lambda i: (i, 0)), whole_spec),
+        in_specs=[vmem, anywhere, vmem, vmem],
+        limit=60,
+        out_specs=(anywhere, anywhere),
     )(sums, weight, basis, right)
 
 
@@ -238,7 +251,7 @@
     )
     piece = exchange(pieces, "z").sum(0)
     both = lax.all_gather(piece, "z")
-    scratch = [(2, half, half), (half, half), (2 * cols, half)]
+    scratch = [(2, half, half), (half, half), (2 * cols, half), (2, 72, half)]
     inverse, right_factor, sums = whole(
         functools.partial(right_kernel, top),
         (f32(rank, rank), f32(cols, rank), f32(2 * nxy, 1, rank)),

time: 156 us -> 153 us (0.981)
  local copies, waits for them, and re-layouts: 4.12 us -> 2.48 us
    pallas_call x1, Pallas kernels: 11.3 us -> 9.08 us  [body(): whole(functools.partial(right_kernel, top), (f32(rank, rank), f32(cols, r...]
    unnamed x12, local copies, waits for them, and re-layouts: 4.11 us -> 2.46 us
where the time goes in v4:
time: 153 us; the launch traced here: 152 us
  blocking collectives  113 us (74%)
  Pallas kernels  17.1 us (11%)
  starting transfers between devices  10.5 us (7%)
  waiting for transfers between devices  6.22 us (4%)
  local copies, waits for them, and re-layouts  2.48 us (2%)
  matrix products  2.43 us (2%)
    all_to_all x4, blocking collectives, exchange(): return lax.all_to_all(blocks, axes, 0, 0)  84.8 us
    all_gather x1, blocking collectives, body(): both = lax.all_gather(piece, 'z')  22.6 us
    all_to_all x1, starting transfers between devices, exchange(): return lax.all_to_all(blocks, axes, 0, 0)  10.5 us
    pallas_call x1, Pallas kernels, body(): whole(functools.partial(right_kernel, top), (f32(rank, rank), f32(cols, r...  9.08 us
    all_to_all x1, waiting for transfers between devices, exchange(): return lax.all_to_all(blocks, axes, 0, 0)  6.22 us
    all_gather x1, blocking collectives, body(): left_factor = lax.all_gather(half, 'core', axis=0, tiled=True)  5.54 us
    pallas_call x1, Pallas kernels, weight_step(): whole(weight_kernel, (f32(rows, cols), f32(cols, rank)), [pltpu.VMEM((cou...  3.72 us
  transfers between devices with their start and end apart: 1, of which 1 were waited for; matrix products, arithmetic and copies ran while one was open for 0% of the time, Pallas kernels for 2%

profile of v4, /device:TPU:1, one launch (start us, length us, event | category | flops | bytes accessed | tf_op | source)
XLA Modules:
  0.0 152.5 jit_solution(7470978997438996457)
XLA Ops:
  0.6 0.0 copy-start
  0.6 1.0 copy-done
  1.7 2.4 %fusion = f32[512,256]{1,0:T(8,128)S(1)} fusion(f32[512,256]{1,0:T(8,128)S(1)} %copy-done, bf16[512,512]{1,0:T(8,128)(2,1)} %gradient_ref.3, f32[512,512]{1,0:T(8,128)} %momentum_ref.3), kind=kOutput, calls=%fused_computation | convolution fusion | flops 806092800 | bytes 2621440 | tf_op jit(solution)/shard_map/dot_general | solution.py:241
  4.1 14.3 %all_to_all.25 = f32[2,256,256]{2,1,0:T(8,128)S(1)} all-to-all(f32[2,256,256]{2,1,0:T(8,128)S(1)} %bitcast.6), channel_id=1, replica_groups=mesh['z'=12,'x'=4,'y'=8,'core'=2] {'core'}, dimensions={0} | all-to-all | bytes 1048576 | tf_op jit(solution)/shard_map/all_to_all | solution.py:228
  18.4 13.2 %all_to_all.26 = f32[32,8,256]{2,1,0:T(8,128)S(1)} all-to-all(f32[32,8,256]{2,1,0:T(8,128)S(1)} %bitcast.8), channel_id=1, replica_groups=mesh['z'=12,'x'=4,'y'=8,'core'=2] {'x','y'}, dimensions={0} | all-to-all | bytes 524288 | tf_op jit(solution)/shard_map/all_to_all | solution.py:228
  31.6 0.0 copy-start.1
  31.7 16.1 %all_to_all.27 = f32[32,8,256]{2,1,0:T(8,128)S(1)} all-to-all(f32[32,8,256]{2,1,0:T(8,128)S(1)} %broadcast_in_dim.2), channel_id=1, replica_groups=mesh['z'=12,'x'=4,'y'=8,'core'=2] {'x','y'}, dimensions={0} | all-to-all | bytes 524288 | tf_op jit(solution)/shard_map/all_to_all | solution.py:228
  47.8 0.0 copy-start.2
  47.8 5.5 %all_gather.9.left_ref = f32[512,256]{1,0:T(8,128)S(1)} all-gather(f32[256,256]{1,0:T(8,128)S(1)} %bitcast.7), channel_id=1, replica_groups=mesh['z'=12,'x'=4,'y'=8,'core'=2] {'core'}, dimensions={0}, use_global_device_ids=true | all-gather | bytes 786432 | tf_op jit(solution)/shard_map/all_gather | solution.py:245
  53.3 0.0 copy-done.1
  53.3 0.0 copy-done.2
  53.3 1.5 shard_map.67
  54.9 41.3 %all_to_all.28 = f32[12,120,128]{2,1,0:T(8,128)S(1)} all-to-all(f32[12,120,128]{2,1,0:T(8,128)S(1)} %shard_map.67), channel_id=1, replica_groups=mesh['z'=12,'x'=4,'y'=8,'core'=2] {'z'}, dimensions={0} | all-to-all | bytes 1474560 | tf_op jit(solution)/shard_map/all_to_all | solution.py:228
  96.2 22.6 %all-gather = f32[1440,128]{1,0:T(8,128)S(1)} all-gather(f32[120,128]{1,0:T(8,128)S(1)} %reduce_sum.29), channel_id=2, replica_groups=mesh['z'=12,'x'=4,'y'=8,'core'=2] {'z'}, dimensions={0}, use_global_device_ids=true | all-gather | bytes 798720 | tf_op jit(solution)/shard_map/all_gather | solution.py:253
  118.8 9.1 %shard_map.68 = (f32[256,256]{1,0:T(8,128)S(1)}, f32[512,256]{1,0:T(8,128)S(1)}, f32[64,1,256]{2,1,0:T(1,128)}) custom-call(f32[12,120,128]{2,1,0:T(8,128)S(1)} %bitcast.5), custom_call_target="tpu_custom_call" | custom-call | flops 10000000000 | bytes 33554432 | tf_op jit(solution)/shard_map/pallas_call | solution.py:255
  127.9 0.0 copy-start.3
  127.9 10.5 %all-to-all-start.4 = ((f32[64,1,256]{2,1,0:T(1,128)}), f32[64,1,256]{2,1,0:T(1,128)S(1)}, u32[]{:S(2)}, u32[]{:S(2)}) async-start(f32[64,1,256]{2,1,0:T(1,128)} %get-tuple-element.10), calls=%async_computation.4 | async-start | bytes 131072 | tf_op jit(solution)/shard_map/all_to_all | solution.py:228
  138.4 2.8 %shard_map.69 = (f32[512,512]{1,0:T(8,128)}, f32[512,256]{1,0:T(8,128)S(1)}) custom-call(f32[256,256]{1,0:T(8,128)S(1)} %get-tuple-element.11.inv_ref, f32[512,256]{1,0:T(8,128)S(1)} %all_gather.9.left_ref, f32[512,256]{1,0:T(8,128)S(1)} %get-tuple-element.12.right_ref, f32[512,512]{1,0:T(8,128)S(1)} %copy-done.1, bf16[512,512]{1,0:T(8,128)(2,1)S(1)} %copy-done.2), custom_call_target="tpu_custom_call" | custom-call | flops 1000000000 | bytes 16777216 | tf_op jit(solution)/shard_map/pallas_call | solution.py:262
  141.1 0.0 copy-done.3
  141.1 0.0 copy-start.4
  141.1 0.8 copy-done.4
  141.9 6.2 %all-to-all-done.4.sums_ref = f32[64,1,256]{2,1,0:T(1,128)S(1)} async-done(((f32[64,1,256]{2,1,0:T(1,128)}), f32[64,1,256]{2,1,0:T(1,128)S(1)}, u32[]{:S(2)}, u32[]{:S(2)}) %all-to-all-start.4) | async-done | bytes 65568 | tf_op jit(solution)/shard_map/all_to_all | solution.py:228
  148.2 0.0 copy-start.5
  148.2 0.6 copy-done.5
  148.8 3.7 %shard_map.70 = (f32[512,512]{1,0:T(8,128)}, f32[512,256]{1,0:T(8,128)}) custom-call(f32[64,1,256]{2,1,0:T(1,128)} %copy-done.5, f32[512,512]{1,0:T(8,128)} %weight_ref.1, f32[512,256]{1,0:T(8,128)} %copy-done.4, f32[512,256]{1,0:T(8,128)} %copy-done.3), custom_call_target="tpu_custom_call" | custom-call | flops 1000000000 | bytes 4194304 | tf_op jit(solution)/shard_map/pallas_call | solution.py:212
  (4 shorter events, 0.1 us)
Async XLA Ops:
  0.6 1.0 copy-start
  31.6 21.7 %copy-start.1 = (f32[512,512]{1,0:T(8,128)S(1)}, f32[512,512]{1,0:T(8,128)}, u32[]{:S(2)}) copy-start(f32[512,512]{1,0:T(8,128)} %momentum_ref.3) | copy-start | bytes 3145732
  47.8 5.5 %copy-start.2 = (bf16[512,512]{1,0:T(8,128)(2,1)S(1)}, bf16[512,512]{1,0:T(8,128)(2,1)}, u32[]{:S(2)}) copy-start(bf16[512,512]{1,0:T(8,128)(2,1)} %gradient_ref.3) | copy-start | bytes 1572868
  127.9 13.2 %copy-start.3 = (f32[512,256]{1,0:T(8,128)}, f32[512,256]{1,0:T(8,128)S(1)}, u32[]{:S(2)}) copy-start(f32[512,256]{1,0:T(8,128)S(1)} %get-tuple-element.12.right_ref) | copy-start | bytes 1572868
  127.9 20.3 %all-to-all-start.4 = ((f32[64,1,256]{2,1,0:T(1,128)}), f32[64,1,256]{2,1,0:T(1,128)S(1)}, u32[]{:S(2)}, u32[]{:S(2)}) async-start(f32[64,1,256]{2,1,0:T(1,128)} %get-tuple-element.10), calls=%async_computation.4 | async-start | bytes 131072 | tf_op jit(solution)/shard_map/all_to_all | solution.py:228
  141.1 0.8 copy-start.4
  148.2 0.6 copy-start.5

commit v5 on v4

--- a/solution.py
+++ b/solution.py
@@ -87,11 +87,14 @@
     nz, low = both_ref.shape[0], both_ref.shape[1] - top
     cols = right_ref.shape[0]
     parts = (block_ref.at[0], cross_ref, block_ref.at[1])
+    low, half = low // 2, n // 2
     for at in range(nz):
         for i in range(0, low, 8):
             row = at * low + i
-            if row < 3 * n:
-                parts[row // n][row % n : row % n + 8, :] = both_ref[at, top + i : top + i + 8, :]
+            if row < 3 * half:
+                for core in range(2):
+                    to, place = row % half + core * half, top + core * low + i
+                    parts[row // half][to : to + 8, :] = both_ref[at, place : place + 8, :]
         stop = min(2 * cols, (at + 1) * top)
         if at * top < stop:
             turned_ref[at * top : stop, :] = both_ref[at, : stop - at * top, :]
@@ -142,13 +145,17 @@
     return jax.ShapeDtypeStruct(shape, jnp.float32)
 
 
-def turn_kernel(top, momentum_ref, gradient_ref, left_ref, out_ref):
+def turn_kernel(top, core_ref, momentum_ref, gradient_ref, left_ref, out_ref, gram_ref):
     nz, both, n = out_ref.shape
-    low = both - top
+    low, half = both - top, n // 2
     cols = momentum_ref.shape[1]
     left = left_ref[...]
     square = mul_tn(left, left)
-    blocks = (square[:n, :n], square[n:, :n], square[n:, n:])
+    gram_ref[:n, :] = square[:n, :n]
+    gram_ref[n : 2 * n, :] = square[n:, :n]
+    gram_ref[2 * n :, :] = square[n:, n:]
+    mine = pl.multiple_of(core_ref[0] * half, half)
+    blocks = [gram_ref[pl.ds(block * n + mine, half), :] for block in range(3)]
     buffer = momentum_decay * momentum_ref[...] + gradient_ref[...].astype(jnp.float32)
     turned = mul_tn(buffer, left)
     for at in range(nz):
@@ -161,8 +168,8 @@
             out_ref[at, fill:top, :] = jnp.zeros((top - fill, n), jnp.float32)
         for i in range(0, low, 8):
             row = at * low + i
-            if row < 3 * n:
-                out_ref[at, top + i : top + i + 8, :] = blocks[row // n][row % n : row % n + 8, :]
+            if row < 3 * half:
+                out_ref[at, top + i : top + i + 8, :] = blocks[row // half][row % half : row % half + 8, :]
             else:
                 out_ref[at, top + i : top + i + 8, :] = jnp.zeros((8, n), jnp.float32)
 
@@ -237,20 +244,33 @@
     nz, nxy = lax.axis_size("z"), lax.axis_size("x") * lax.axis_size("y")
     rows, cols = momentum.shape
     rank = right_basis.shape[1]
-    buffer = momentum_decay * momentum + gradient.astype(jnp.float32)
-    partial = jnp.dot(buffer, right_basis, precision=highest)
-    half = exchange(partial.reshape(2, rows // 2, rank), "core").sum(0)
+    core = lax.axis_index("core")
+
+    def product(at):
+        rows_of = functools.partial(lax.dynamic_slice_in_dim, start_index=at * (rows // 2), slice_size=rows // 2)
+        buffer = momentum_decay * rows_of(momentum) + rows_of(gradient).astype(jnp.float32)
+        return jnp.dot(buffer, right_basis, precision=highest)
+
+    sent, own = lax.optimization_barrier(
+        (lax.ppermute(product(1 - core), "core", [(0, 1), (1, 0)]), product(core))
+    )
+    half = sent + own
     share = exchange(half.reshape(nxy, rows // (2 * nxy), rank), PLANE).sum(0)
     half = spread(share, PLANE, nxy).reshape(rows // 2, rank)
     left_factor = lax.all_gather(half, "core", axis=0, tiled=True)
     half = rank // 2
     top = -(-2 * cols // (8 * nz)) * 8
-    low = -(-3 * half // (8 * nz)) * 8
-    pieces = whole(functools.partial(turn_kernel, top), f32(nz, top + low, half))(
-        momentum, gradient, left_factor
-    )
+    low = -(-3 * half // (16 * nz)) * 8
+    vmem = pl.BlockSpec(memory_space=pltpu.VMEM)
+    pieces = whole(
+        functools.partial(turn_kernel, top),
+        f32(nz, top + low, half),
+        [pltpu.VMEM((3 * half, half), jnp.float32)],
+        in_specs=[pl.BlockSpec(memory_space=pltpu.SMEM), vmem, vmem, vmem],
+    )(core.reshape(1), momentum, gradient, left_factor)
     piece = exchange(pieces, "z").sum(0)
-    both = lax.all_gather(piece, "z")
+    shares = lax.all_gather(piece[top:], "core", axis=0, tiled=True)
+    both = lax.all_gather(jnp.concatenate([piece[:top], shares], axis=0), "z")
     scratch = [(2, half, half), (half, half), (2 * cols, half), (2, 72, half)]
     inverse, right_factor, sums = whole(
         functools.partial(right_kernel, top),

time: 153 us -> 150 us (0.980)
  blocking collectives: 113 us -> 97.5 us
  starting transfers between devices: 10.5 us -> 22.5 us
    all_to_all x4 -> x3, blocking collectives: 84.8 us -> 67.3 us  [exchange(): return lax.all_to_all(blocks, axes, 0, 0)]
    ppermute x0 -> x1, starting transfers between devices: none -> 12.4 us  [body(): lax.ppermute(product(1 - core), 'core', [(0, 1), (1, 0)])]
    all_gather x1 -> x2, blocking collectives: 22.6 us -> 24.8 us  [the longest x1 20.4 us: body(): both = lax.all_gather(jnp.concatenate([piece[:top], shares], axis=0), 'z')]
  transfers between devices with their start and end apart: 1 -> 2, of which waited for: 1 -> 2; matrix products, arithmetic and copies ran while one was open for 0% -> 0% of each run, Pallas kernels for 2% -> 2%
where the time goes in v5:
time: 150 us
  blocking collectives  97.5 us (65%)
  starting transfers between devices  22.5 us (15%)
  Pallas kernels  17.1 us (11%)
  waiting for transfers between devices  6.7 us (4%)
  local copies, waits for them, and re-layouts  2.48 us (2%)
  matrix products  2.42 us (2%)
    all_to_all x3, blocking collectives, exchange(): return lax.all_to_all(blocks, axes, 0, 0)  67.3 us
    all_gather x1, blocking collectives, body(): both = lax.all_gather(jnp.concatenate([piece[:top], shares], axis=0), 'z')  20.4 us
    ppermute x1, starting transfers between devices, body(): lax.ppermute(product(1 - core), 'core', [(0, 1), (1, 0)])  12.4 us
    all_to_all x1, starting transfers between devices, exchange(): return lax.all_to_all(blocks, axes, 0, 0)  10.1 us
    pallas_call x1, Pallas kernels, body(): whole(functools.partial(right_kernel, top), (f32(rank, rank), f32(cols, r...  9.08 us
    all_to_all x1, waiting for transfers between devices, exchange(): return lax.all_to_all(blocks, axes, 0, 0)  6.22 us
    all_gather x1, blocking collectives, body(): left_factor = lax.all_gather(half, 'core', axis=0, tiled=True)  5.41 us
    all_gather x1, blocking collectives, body(): shares = lax.all_gather(piece[top:], 'core', axis=0, tiled=True)  4.39 us
  transfers between devices with their start and end apart: 2, of which 2 were waited for; matrix products, arithmetic and copies ran while one was open for 0% of the time, Pallas kernels for 2%

profile of v5, /device:TPU:1, one launch (start us, length us, event | category | flops | bytes accessed | tf_op | source)
XLA Modules:
  0.0 149.5 jit_solution(10433462775953665737)
XLA Ops:
  0.6 0.0 copy-start
  0.6 0.0 copy-start.1
  0.7 1.0 copy-done
  1.7 0.0 copy-start.2
  1.7 1.8 %fusion.5 = f32[256,256]{1,0:T(8,128)S(1)} fusion(f32[512,256]{1,0:T(8,128)S(1)} %copy-done, f32[512,512]{1,0:T(8,128)} %momentum_ref.3, s32[]{:T(128)S(6)} %select_n.8, bf16[512,512]{1,0:T(8,128)(2,1)} %gradient_ref.3), kind=kOutput, calls=%fused_computation.5 | convolution fusion | flops 403046400 | bytes 1572868 | tf_op jit(solution)/shard_map/dot_general | solution.py:252
  3.5 12.4 %collective-permute-start = (f32[256,256]{1,0:T(8,128)S(1)}, f32[256,256]{1,0:T(8,128)S(1)}, u32[]{:S(2)}, u32[]{:S(2)}) collective-permute-start(f32[256,256]{1,0:T(8,128)S(1)} %fusion.5), channel_id=1, source_target_pairs={{0,1},{1,0},{2,3},{3,2},{4,5},{5,4},{6,7},{7,6},{8,9},{9,8},{10,11... | collective-permute-start | bytes 786440 | tf_op jit(solution)/shard_map/ppermute | solution.py:255
  15.9 0.0 copy-done.1
  15.9 0.0 copy-done.2
  15.9 0.6 fusion
  16.6 0.5 collective-permute-done
  17.1 13.2 %all_to_all.20 = f32[32,8,256]{2,1,0:T(8,128)S(1)} all-to-all(f32[32,8,256]{2,1,0:T(8,128)S(1)} %add_bitcast_fusion), channel_id=1, replica_groups=mesh['z'=12,'x'=4,'y'=8,'core'=2] {'x','y'}, dimensions={0} | all-to-all | bytes 524288 | tf_op jit(solution)/shard_map/all_to_all | solution.py:235
  30.3 16.0 %all_to_all.21 = f32[32,8,256]{2,1,0:T(8,128)S(1)} all-to-all(f32[32,8,256]{2,1,0:T(8,128)S(1)} %broadcast_in_dim.2), channel_id=1, replica_groups=mesh['z'=12,'x'=4,'y'=8,'core'=2] {'x','y'}, dimensions={0} | all-to-all | bytes 524288 | tf_op jit(solution)/shard_map/all_to_all | solution.py:235
  46.3 5.4 %all_gather.12.left_ref = f32[512,256]{1,0:T(8,128)S(1)} all-gather(f32[256,256]{1,0:T(8,128)S(1)} %bitcast.8), channel_id=1, replica_groups=mesh['z'=12,'x'=4,'y'=8,'core'=2] {'core'}, dimensions={0}, use_global_device_ids=true | all-gather | bytes 786432 | tf_op jit(solution)/shard_map/all_gather | solution.py:260
  51.7 1.5 %shard_map.67 = f32[12,104,128]{2,1,0:T(8,128)S(1)} custom-call(s32[1]{0:T(128)} %bitcast.core_ref, f32[512,512]{1,0:T(8,128)S(1)} %copy-done.1, bf16[512,512]{1,0:T(8,128)(2,1)S(1)} %copy-done.2, f32[512,256]{1,0:T(8,128)S(1)} %all_gather.12.left_ref), custom_call_target="tpu_custom_call" | custom-call | flops 1000000000 | bytes 4194304 | tf_op jit(solution)/shard_map/pallas_call | solution.py:265
  53.2 38.2 %all_to_all.22 = f32[12,104,128]{2,1,0:T(8,128)S(1)} all-to-all(f32[12,104,128]{2,1,0:T(8,128)S(1)} %shard_map.67), channel_id=1, replica_groups=mesh['z'=12,'x'=4,'y'=8,'core'=2] {'z'}, dimensions={0} | all-to-all | bytes 1277952 | tf_op jit(solution)/shard_map/all_to_all | solution.py:235
  91.5 4.4 %all_gather.13 = f32[32,128]{1,0:T(8,128)S(1)} all-gather(f32[16,128]{1,0:T(8,128)S(1)} %slice.9), channel_id=1, replica_groups=mesh['z'=12,'x'=4,'y'=8,'core'=2] {'core'}, dimensions={0}, use_global_device_ids=true | all-gather | bytes 24576 | tf_op jit(solution)/shard_map/all_gather | solution.py:272
  95.9 20.4 %all-gather = f32[1440,128]{1,0:T(8,128)S(1)} all-gather(f32[120,128]{1,0:T(8,128)S(1)} %pad_maximum_fusion), channel_id=2, replica_groups=mesh['z'=12,'x'=4,'y'=8,'core'=2] {'z'}, dimensions={0}, use_global_device_ids=true | all-gather | bytes 798720 | tf_op jit(solution)/shard_map/all_gather | solution.py:273
  116.2 9.1 %shard_map.68 = (f32[256,256]{1,0:T(8,128)S(1)}, f32[512,256]{1,0:T(8,128)S(1)}, f32[64,1,256]{2,1,0:T(1,128)}) custom-call(f32[12,120,128]{2,1,0:T(8,128)S(1)} %bitcast.7), custom_call_target="tpu_custom_call" | custom-call | flops 10000000000 | bytes 33554432 | tf_op jit(solution)/shard_map/pallas_call | solution.py:275
  125.3 0.0 copy-start.3
  125.3 10.1 %all-to-all-start.3 = ((f32[64,1,256]{2,1,0:T(1,128)}), f32[64,1,256]{2,1,0:T(1,128)S(1)}, u32[]{:S(2)}, u32[]{:S(2)}) async-start(f32[64,1,256]{2,1,0:T(1,128)} %get-tuple-element.14), calls=%async_computation.3 | async-start | bytes 131072 | tf_op jit(solution)/shard_map/all_to_all | solution.py:235
  135.4 2.8 %shard_map.69 = (f32[512,512]{1,0:T(8,128)}, f32[512,256]{1,0:T(8,128)S(1)}) custom-call(f32[256,256]{1,0:T(8,128)S(1)} %get-tuple-element.15.inv_ref, f32[512,256]{1,0:T(8,128)S(1)} %all_gather.12.left_ref, f32[512,256]{1,0:T(8,128)S(1)} %get-tuple-element.16.right_ref, f32[512,512]{1,0:T(8,128)S(1)} %copy-done.1, bf16[512,512]{1,0:T(8,128)(2,1)S(1)} %copy-done.2), custom_call_target="tpu_custom_call" | custom-call | flops 1000000000 | bytes 16777216 | tf_op jit(solution)/shard_map/pallas_call | solution.py:282
  138.2 0.0 copy-done.3
  138.2 0.0 copy-start.4
  138.2 0.8 copy-done.4
  139.0 6.2 %all-to-all-done.3.sums_ref = f32[64,1,256]{2,1,0:T(1,128)S(1)} async-done(((f32[64,1,256]{2,1,0:T(1,128)}), f32[64,1,256]{2,1,0:T(1,128)S(1)}, u32[]{:S(2)}, u32[]{:S(2)}) %all-to-all-start.3) | async-done | bytes 65568 | tf_op jit(solution)/shard_map/all_to_all | solution.py:235
  145.2 0.0 copy-start.5
  145.2 0.6 copy-done.5
  145.8 3.7 %shard_map.70 = (f32[512,512]{1,0:T(8,128)}, f32[512,256]{1,0:T(8,128)}) custom-call(f32[64,1,256]{2,1,0:T(1,128)} %copy-done.5, f32[512,512]{1,0:T(8,128)} %weight_ref.1, f32[512,256]{1,0:T(8,128)} %copy-done.4, f32[512,256]{1,0:T(8,128)} %copy-done.3), custom_call_target="tpu_custom_call" | custom-call | flops 1000000000 | bytes 4194304 | tf_op jit(solution)/shard_map/pallas_call | solution.py:219
  (7 shorter events, 0.1 us)
Async XLA Ops:
  0.6 1.0 copy-start
  0.6 15.3 %copy-start.1 = (f32[512,512]{1,0:T(8,128)S(1)}, f32[512,512]{1,0:T(8,128)}, u32[]{:S(2)}) copy-start(f32[512,512]{1,0:T(8,128)} %momentum_ref.3) | copy-start | bytes 3145732
  1.7 14.2 %copy-start.2 = (bf16[512,512]{1,0:T(8,128)(2,1)S(1)}, bf16[512,512]{1,0:T(8,128)(2,1)}, u32[]{:S(2)}) copy-start(bf16[512,512]{1,0:T(8,128)(2,1)} %gradient_ref.3) | copy-start | bytes 1572868
  3.5 13.6 %collective-permute-start = (f32[256,256]{1,0:T(8,128)S(1)}, f32[256,256]{1,0:T(8,128)S(1)}, u32[]{:S(2)}, u32[]{:S(2)}) collective-permute-start(f32[256,256]{1,0:T(8,128)S(1)} %fusion.5), channel_id=1, source_target_pairs={{0,1},{1,0},{2,3},{3,2},{4,5},{5,4},{6,7},{7,6},{8,9},{9,8},{10,11... | collective-permute-start | bytes 786440 | tf_op jit(solution)/shard_map/ppermute | solution.py:255
  125.3 12.9 %copy-start.3 = (f32[512,256]{1,0:T(8,128)}, f32[512,256]{1,0:T(8,128)S(1)}, u32[]{:S(2)}) copy-start(f32[512,256]{1,0:T(8,128)S(1)} %get-tuple-element.16.right_ref) | copy-start | bytes 1572868
  125.3 19.9 %all-to-all-start.3 = ((f32[64,1,256]{2,1,0:T(1,128)}), f32[64,1,256]{2,1,0:T(1,128)S(1)}, u32[]{:S(2)}, u32[]{:S(2)}) async-start(f32[64,1,256]{2,1,0:T(1,128)} %get-tuple-element.14), calls=%async_computation.3 | async-start | bytes 131072 | tf_op jit(solution)/shard_map/all_to_all | solution.py:235
  138.2 0.8 copy-start.4
  145.2 0.6 copy-start.5

commit v6 on v5

--- a/solution.py
+++ b/solution.py
@@ -188,45 +188,53 @@
     new_momentum_ref[...] = buffer - (1.0 - momentum_decay) * products(basis, halves_of(right_ref[...]))
 
 
-def weight_kernel(sums_ref, weight_ref, basis_ref, right_ref, new_weight_ref, new_right_ref, block_ref, scaled_ref, in_sems, out_sems):
+def weight_kernel(*refs):
+    sums_ref, weight_ref, basis_ref, right_ref, new_weight_ref, new_right_ref, block_ref, near_ref, basis_near, right_near = refs[:10]
+    in_sems, out_sems = refs[10:]
     count, size = block_ref.shape[:2]
     rows = [pl.ds(i * size, size) for i in range(count)]
-    loads = [pltpu.make_async_copy(weight_ref.at[rows[i]], block_ref.at[i], in_sems.at[i]) for i in range(count)]
-    stores = [pltpu.make_async_copy(block_ref.at[i], new_weight_ref.at[rows[i]], out_sems.at[i]) for i in range(count)]
+    pairs = [(sums_ref, near_ref), (right_ref, right_near), (basis_ref, basis_near)]
+    pairs += [(weight_ref.at[rows[i]], block_ref.at[i]) for i in range(count)]
+    loads = [pltpu.make_async_copy(*pair, in_sems.at[i]) for i, pair in enumerate(pairs)]
     for load in loads:
         load.start()
-    scale = lax.rsqrt(jnp.sum(sums_ref[...], axis=0) / COLS + epsilon_rms)
-    new_right = right_ref[...] * scale
-    scaled_ref[...] = new_right
-    last = pltpu.make_async_copy(scaled_ref, new_right_ref, out_sems.at[count])
-    last.start()
+    stores = [pltpu.make_async_copy(block_ref.at[i], new_weight_ref.at[rows[i]], out_sems.at[i]) for i in range(count)]
+    stores.append(pltpu.make_async_copy(right_near, new_right_ref, out_sems.at[count]))
+    loads[0].wait()
+    scale = lax.rsqrt(jnp.sum(near_ref[...], axis=0) / COLS + epsilon_rms)
+    loads[1].wait()
+    new_right = right_near[...] * scale
+    right_near[...] = new_right
+    stores[count].start()
     scaled = halves_of(new_right)
+    loads[2].wait()
     for i in range(count):
-        product = products(basis_ref[rows[i], :], scaled)
-        loads[i].wait()
+        product = products(basis_near[rows[i], :], scaled)
+        loads[3 + i].wait()
         block_ref[i] = block_ref[i] - step_size * product
         stores[i].start()
     for store in stores:
         store.wait()
-    last.wait()
 
 
 def weight_step(sums, weight, basis, right):
     rows, cols = weight.shape
     rank = right.shape[1]
-    count = 2
-    vmem, anywhere = pl.BlockSpec(memory_space=pltpu.VMEM), pl.BlockSpec(memory_space=pl.ANY)
+    count = 1
+    anywhere = pl.BlockSpec(memory_space=pl.ANY)
     return whole(
         weight_kernel,
         (f32(rows, cols), f32(cols, rank)),
         [
             pltpu.VMEM((count, rows // count, cols), jnp.float32),
-            pltpu.VMEM((cols, rank), jnp.float32),
-            pltpu.SemaphoreType.DMA((count,)),
+            pltpu.VMEM(sums.shape, jnp.float32),
+            pltpu.VMEM(basis.shape, jnp.float32),
+            pltpu.VMEM(right.shape, jnp.float32),
+            pltpu.SemaphoreType.DMA((count + 3,)),
             pltpu.SemaphoreType.DMA((count + 1,)),
         ],
-        in_specs=[vmem, anywhere, vmem, vmem],
         limit=60,
+        in_specs=[anywhere] * 4,
         out_specs=(anywhere, anywhere),
     )(sums, weight, basis, right)
 

time: 150 us -> 149 us (level)
  no operation moved by 1% of the time
where the time goes in v6:
time: 149 us
  blocking collectives  97.5 us (65%)
  starting transfers between devices  22.5 us (15%)
  Pallas kernels  16.3 us (11%)
  waiting for transfers between devices  6.7 us (4%)
  local copies, waits for them, and re-layouts  2.48 us (2%)
  matrix products  2.42 us (2%)
    all_to_all x3, blocking collectives, exchange(): return lax.all_to_all(blocks, axes, 0, 0)  67.3 us
    all_gather x1, blocking collectives, body(): both = lax.all_gather(jnp.concatenate([piece[:top], shares], axis=0), 'z')  20.4 us
    ppermute x1, starting transfers between devices, body(): lax.ppermute(product(1 - core), 'core', [(0, 1), (1, 0)])  12.4 us
    all_to_all x1, starting transfers between devices, exchange(): return lax.all_to_all(blocks, axes, 0, 0)  10.1 us
    pallas_call x1, Pallas kernels, body(): whole(functools.partial(right_kernel, top), (f32(rank, rank), f32(cols, r...  9.08 us
    all_to_all x1, waiting for transfers between devices, exchange(): return lax.all_to_all(blocks, axes, 0, 0)  6.22 us
    all_gather x1, blocking collectives, body(): left_factor = lax.all_gather(half, 'core', axis=0, tiled=True)  5.41 us
    all_gather x1, blocking collectives, body(): shares = lax.all_gather(piece[top:], 'core', axis=0, tiled=True)  4.39 us
  transfers between devices with their start and end apart: 2, of which 2 were waited for; matrix products, arithmetic and copies ran while one was open for 0% of the time, Pallas kernels for 2%

profile of v6, /device:TPU:1, one launch (start us, length us, event | category | flops | bytes accessed | tf_op | source)
XLA Modules:
  0.0 148.8 jit_solution(4303058709810854024)
XLA Ops:
  0.6 0.0 copy-start
  0.6 0.0 copy-start.1
  0.7 1.0 copy-done
  1.7 0.0 copy-start.2
  1.7 1.8 %fusion.5 = f32[256,256]{1,0:T(8,128)S(1)} fusion(f32[512,256]{1,0:T(8,128)S(1)} %copy-done, f32[512,512]{1,0:T(8,128)} %momentum_ref.3, s32[]{:T(128)S(6)} %select_n.8, bf16[512,512]{1,0:T(8,128)(2,1)} %gradient_ref.3), kind=kOutput, calls=%fused_computation.5 | convolution fusion | flops 403046400 | bytes 1572868 | tf_op jit(solution)/shard_map/dot_general | solution.py:260
  3.5 12.4 %collective-permute-start = (f32[256,256]{1,0:T(8,128)S(1)}, f32[256,256]{1,0:T(8,128)S(1)}, u32[]{:S(2)}, u32[]{:S(2)}) collective-permute-start(f32[256,256]{1,0:T(8,128)S(1)} %fusion.5), channel_id=1, source_target_pairs={{0,1},{1,0},{2,3},{3,2},{4,5},{5,4},{6,7},{7,6},{8,9},{9,8},{10,11... | collective-permute-start | bytes 786440 | tf_op jit(solution)/shard_map/ppermute | solution.py:263
  15.9 0.0 copy-done.1
  15.9 0.0 copy-done.2
  15.9 0.6 fusion
  16.6 0.5 collective-permute-done
  17.1 13.2 %all_to_all.20 = f32[32,8,256]{2,1,0:T(8,128)S(1)} all-to-all(f32[32,8,256]{2,1,0:T(8,128)S(1)} %add_bitcast_fusion), channel_id=1, replica_groups=mesh['z'=12,'x'=4,'y'=8,'core'=2] {'x','y'}, dimensions={0} | all-to-all | bytes 524288 | tf_op jit(solution)/shard_map/all_to_all | solution.py:243
  30.3 16.0 %all_to_all.21 = f32[32,8,256]{2,1,0:T(8,128)S(1)} all-to-all(f32[32,8,256]{2,1,0:T(8,128)S(1)} %broadcast_in_dim.2), channel_id=1, replica_groups=mesh['z'=12,'x'=4,'y'=8,'core'=2] {'x','y'}, dimensions={0} | all-to-all | bytes 524288 | tf_op jit(solution)/shard_map/all_to_all | solution.py:243
  46.3 5.4 %all_gather.12.left_ref = f32[512,256]{1,0:T(8,128)S(1)} all-gather(f32[256,256]{1,0:T(8,128)S(1)} %bitcast.8), channel_id=1, replica_groups=mesh['z'=12,'x'=4,'y'=8,'core'=2] {'core'}, dimensions={0}, use_global_device_ids=true | all-gather | bytes 786432 | tf_op jit(solution)/shard_map/all_gather | solution.py:268
  51.7 1.5 %shard_map.67 = f32[12,104,128]{2,1,0:T(8,128)S(1)} custom-call(s32[1]{0:T(128)} %bitcast.core_ref, f32[512,512]{1,0:T(8,128)S(1)} %copy-done.1, bf16[512,512]{1,0:T(8,128)(2,1)S(1)} %copy-done.2, f32[512,256]{1,0:T(8,128)S(1)} %all_gather.12.left_ref), custom_call_target="tpu_custom_call" | custom-call | flops 1000000000 | bytes 4194304 | tf_op jit(solution)/shard_map/pallas_call | solution.py:273
  53.2 38.2 %all_to_all.22 = f32[12,104,128]{2,1,0:T(8,128)S(1)} all-to-all(f32[12,104,128]{2,1,0:T(8,128)S(1)} %shard_map.67), channel_id=1, replica_groups=mesh['z'=12,'x'=4,'y'=8,'core'=2] {'z'}, dimensions={0} | all-to-all | bytes 1277952 | tf_op jit(solution)/shard_map/all_to_all | solution.py:243
  91.5 4.4 %all_gather.13 = f32[32,128]{1,0:T(8,128)S(1)} all-gather(f32[16,128]{1,0:T(8,128)S(1)} %slice.9), channel_id=1, replica_groups=mesh['z'=12,'x'=4,'y'=8,'core'=2] {'core'}, dimensions={0}, use_global_device_ids=true | all-gather | bytes 24576 | tf_op jit(solution)/shard_map/all_gather | solution.py:280
  95.9 20.4 %all-gather = f32[1440,128]{1,0:T(8,128)S(1)} all-gather(f32[120,128]{1,0:T(8,128)S(1)} %pad_maximum_fusion), channel_id=2, replica_groups=mesh['z'=12,'x'=4,'y'=8,'core'=2] {'z'}, dimensions={0}, use_global_device_ids=true | all-gather | bytes 798720 | tf_op jit(solution)/shard_map/all_gather | solution.py:281
  116.2 9.1 %shard_map.68 = (f32[256,256]{1,0:T(8,128)S(1)}, f32[512,256]{1,0:T(8,128)S(1)}, f32[64,1,256]{2,1,0:T(1,128)}) custom-call(f32[12,120,128]{2,1,0:T(8,128)S(1)} %bitcast.7), custom_call_target="tpu_custom_call" | custom-call | flops 10000000000 | bytes 33554432 | tf_op jit(solution)/shard_map/pallas_call | solution.py:283
  125.3 0.0 copy-start.3
  125.3 10.1 %all-to-all-start.3 = ((f32[64,1,256]{2,1,0:T(1,128)}), f32[64,1,256]{2,1,0:T(1,128)S(1)}, u32[]{:S(2)}, u32[]{:S(2)}) async-start(f32[64,1,256]{2,1,0:T(1,128)} %get-tuple-element.14), calls=%async_computation.3 | async-start | bytes 131072 | tf_op jit(solution)/shard_map/all_to_all | solution.py:243
  135.4 2.8 %shard_map.69 = (f32[512,512]{1,0:T(8,128)}, f32[512,256]{1,0:T(8,128)S(1)}) custom-call(f32[256,256]{1,0:T(8,128)S(1)} %get-tuple-element.15.inv_ref, f32[512,256]{1,0:T(8,128)S(1)} %all_gather.12.left_ref, f32[512,256]{1,0:T(8,128)S(1)} %get-tuple-element.16.right_ref.refs_3_, f32[512,512]{1,0:T(8,128)S(1)} %copy-done.1, bf16[512,512]{1,0:T(8,128)(2,1)S(1)} %copy-done.2), custom_call_target="tpu_custom_call" | custom-call | flops 1000000000 | bytes 16777216 | tf_op jit(solution)/shard_map/pallas_call | solution.py:290
  138.2 0.0 copy-done.3
  138.2 0.0 copy-start.4
  138.2 0.8 copy-done.4
  139.0 6.2 %all-to-all-done.3.refs_0_ = f32[64,1,256]{2,1,0:T(1,128)S(1)} async-done(((f32[64,1,256]{2,1,0:T(1,128)}), f32[64,1,256]{2,1,0:T(1,128)S(1)}, u32[]{:S(2)}, u32[]{:S(2)}) %all-to-all-start.3) | async-done | bytes 65568 | tf_op jit(solution)/shard_map/all_to_all | solution.py:243
  145.2 0.0 copy-start.5
  145.2 0.6 copy-done.5
  145.8 3.0 %shard_map.70 = (f32[512,512]{1,0:T(8,128)}, f32[512,256]{1,0:T(8,128)}) custom-call(f32[64,1,256]{2,1,0:T(1,128)} %copy-done.5, f32[512,512]{1,0:T(8,128)} %refs_1_.1, f32[512,256]{1,0:T(8,128)} %copy-done.4, f32[512,256]{1,0:T(8,128)} %copy-done.3), custom_call_target="tpu_custom_call" | custom-call | flops 1000000000 | bytes 4194304 | tf_op jit(solution)/shard_map/pallas_call | solution.py:225
  (7 shorter events, 0.1 us)
Async XLA Ops:
  0.6 1.0 copy-start
  0.6 15.3 %copy-start.1 = (f32[512,512]{1,0:T(8,128)S(1)}, f32[512,512]{1,0:T(8,128)}, u32[]{:S(2)}) copy-start(f32[512,512]{1,0:T(8,128)} %momentum_ref.3) | copy-start | bytes 3145732
  1.7 14.2 %copy-start.2 = (bf16[512,512]{1,0:T(8,128)(2,1)S(1)}, bf16[512,512]{1,0:T(8,128)(2,1)}, u32[]{:S(2)}) copy-start(bf16[512,512]{1,0:T(8,128)(2,1)} %gradient_ref.3) | copy-start | bytes 1572868
  3.5 13.6 %collective-permute-start = (f32[256,256]{1,0:T(8,128)S(1)}, f32[256,256]{1,0:T(8,128)S(1)}, u32[]{:S(2)}, u32[]{:S(2)}) collective-permute-start(f32[256,256]{1,0:T(8,128)S(1)} %fusion.5), channel_id=1, source_target_pairs={{0,1},{1,0},{2,3},{3,2},{4,5},{5,4},{6,7},{7,6},{8,9},{9,8},{10,11... | collective-permute-start | bytes 786440 | tf_op jit(solution)/shard_map/ppermute | solution.py:263
  125.3 12.9 %copy-start.3 = (f32[512,256]{1,0:T(8,128)}, f32[512,256]{1,0:T(8,128)S(1)}, u32[]{:S(2)}) copy-start(f32[512,256]{1,0:T(8,128)S(1)} %get-tuple-element.16.right_ref.refs_3_) | copy-start | bytes 1572868
  125.3 19.9 %all-to-all-start.3 = ((f32[64,1,256]{2,1,0:T(1,128)}), f32[64,1,256]{2,1,0:T(1,128)S(1)}, u32[]{:S(2)}, u32[]{:S(2)}) async-start(f32[64,1,256]{2,1,0:T(1,128)} %get-tuple-element.14), calls=%async_computation.3 | async-start | bytes 131072 | tf_op jit(solution)/shard_map/all_to_all | solution.py:243
  138.2 0.8 copy-start.4
  145.2 0.6 copy-start.5

commit v7 on v6

--- a/solution.py
+++ b/solution.py
@@ -135,7 +135,7 @@
         kernel,
         out_shape=shapes,
         scratch_shapes=list(scratch),
-        compiler_params=pltpu.CompilerParams(vmem_limit_bytes=limit * 1024 * 1024),
+        compiler_params=pltpu.CompilerParams(vmem_limit_bytes=int(limit * 1024 * 1024)),
         cost_estimate=pl.CostEstimate(flops=cost[0], bytes_accessed=cost[1], transcendentals=0),
         **kw,
     )
@@ -143,6 +143,38 @@
 
 def f32(*shape):
     return jax.ShapeDtypeStruct(shape, jnp.float32)
+
+
+def product_kernel(half_ref, momentum_ref, gradient_ref, right_ref, out_ref, momentum_near, gradient_near, right_near, sems):
+    size = out_ref.shape[0]
+    rows = pl.ds(pl.multiple_of(half_ref[0] * size, size), size)
+    pairs = [(right_ref, right_near), (momentum_ref.at[rows], momentum_near), (gradient_ref.at[rows], gradient_near)]
+    loads = [pltpu.make_async_copy(*pair, sems.at[i]) for i, pair in enumerate(pairs)]
+    for load in loads:
+        load.start()
+    for load in loads:
+        load.wait()
+    buffer = momentum_decay * momentum_near[...] + gradient_near[...].astype(jnp.float32)
+    out_ref[...] = mul(buffer, right_near[...])
+
+
+def product_of(half, momentum, gradient, right):
+    rows, cols = momentum.shape
+    rank = right.shape[1]
+    anywhere = pl.BlockSpec(memory_space=pl.ANY)
+    return whole(
+        product_kernel,
+        f32(rows // 2, rank),
+        [
+            pltpu.VMEM((rows // 2, cols), momentum.dtype),
+            pltpu.VMEM((rows // 2, cols), gradient.dtype),
+            pltpu.VMEM(right.shape, right.dtype),
+            pltpu.SemaphoreType.DMA((3,)),
+        ],
+        limit=53.6,
+        in_specs=[pl.BlockSpec(memory_space=pltpu.SMEM)] + [anywhere] * 3,
+        out_specs=pl.BlockSpec(memory_space=pltpu.VMEM),
+    )(half.reshape(1), momentum, gradient, right)
 
 
 def turn_kernel(top, core_ref, momentum_ref, gradient_ref, left_ref, out_ref, gram_ref):
@@ -233,7 +265,7 @@
             pltpu.SemaphoreType.DMA((count + 3,)),
             pltpu.SemaphoreType.DMA((count + 1,)),
         ],
-        limit=60,
+        limit=53.6,
         in_specs=[anywhere] * 4,
         out_specs=(anywhere, anywhere),
     )(sums, weight, basis, right)
@@ -259,8 +291,9 @@
         buffer = momentum_decay * rows_of(momentum) + rows_of(gradient).astype(jnp.float32)
         return jnp.dot(buffer, right_basis, precision=highest)
 
+    other = product_of(1 - core, momentum, gradient, right_basis)
     sent, own = lax.optimization_barrier(
-        (lax.ppermute(product(1 - core), "core", [(0, 1), (1, 0)]), product(core))
+        (lax.ppermute(other, "core", [(0, 1), (1, 0)]), product(core))
     )
     half = sent + own
     share = exchange(half.reshape(nxy, rows // (2 * nxy), rank), PLANE).sum(0)

time: 149 us -> 148 us (level)
  Pallas kernels: 16.3 us -> 18.5 us
  matrix products: 2.42 us -> 0.63 us
  local copies, waits for them, and re-layouts: 2.48 us -> 0.83 us
    pallas_call x0 -> x1, Pallas kernels: none -> 2.14 us  [product_of(): whole(product_kernel, f32(rows // 2, rank), [pltpu.VMEM((rows // 2, cols)...]
    dot_general x2 -> x1, matrix products: 2.42 us -> 0.63 us  [product(): return jnp.dot(buffer, right_basis, precision=highest)]
    unnamed x12 -> x10, local copies, waits for them, and re-layouts: 2.45 us -> 0.8 us
where the time goes in v7:
time: 148 us
  blocking collectives  97.5 us (66%)
  starting transfers between devices  22.5 us (15%)
  Pallas kernels  18.5 us (12%)
  waiting for transfers between devices  6.7 us (5%)
    all_to_all x3, blocking collectives, exchange(): return lax.all_to_all(blocks, axes, 0, 0)  67.3 us
    all_gather x1, blocking collectives, body(): both = lax.all_gather(jnp.concatenate([piece[:top], shares], axis=0), 'z')  20.4 us
    ppermute x1, starting transfers between devices, body(): lax.ppermute(other, 'core', [(0, 1), (1, 0)])  12.4 us
    all_to_all x1, starting transfers between devices, exchange(): return lax.all_to_all(blocks, axes, 0, 0)  10.1 us
    pallas_call x1, Pallas kernels, body(): whole(functools.partial(right_kernel, top), (f32(rank, rank), f32(cols, r...  9.08 us
    all_to_all x1, waiting for transfers between devices, exchange(): return lax.all_to_all(blocks, axes, 0, 0)  6.22 us
    all_gather x1, blocking collectives, body(): left_factor = lax.all_gather(half, 'core', axis=0, tiled=True)  5.41 us
    all_gather x1, blocking collectives, body(): shares = lax.all_gather(piece[top:], 'core', axis=0, tiled=True)  4.39 us
  transfers between devices with their start and end apart: 2, of which 2 were waited for; matrix products, arithmetic and copies ran while one was open for 0% of the time, Pallas kernels for 2%

profile of v7, /device:TPU:1, one launch (start us, length us, event | category | flops | bytes accessed | tf_op | source)
XLA Modules:
  0.0 147.5 jit_solution(5616133311614224079)
XLA Ops:
  0.6 0.0 copy-start
  0.6 0.0 copy-start.1
  0.7 0.0 copy-start.4
  0.7 2.1 %shard_map.67 = f32[256,256]{1,0:T(8,128)S(1)} custom-call(s32[1]{0:T(128)} %bitcast.1.half_ref, f32[512,512]{1,0:T(8,128)} %momentum_ref.5, bf16[512,512]{1,0:T(8,128)(2,1)} %gradient_ref.5, f32[512,256]{1,0:T(8,128)} %right_ref.1), custom_call_target="tpu_custom_call" | custom-call | flops 1000000000 | bytes 4194304 | tf_op jit(solution)/shard_map/pallas_call | solution.py:165
  2.8 12.4 %collective-permute-start = (f32[256,256]{1,0:T(8,128)S(1)}, f32[256,256]{1,0:T(8,128)S(1)}, u32[]{:S(2)}, u32[]{:S(2)}) collective-permute-start(f32[256,256]{1,0:T(8,128)S(1)} %shard_map.67), channel_id=1, source_target_pairs={{0,1},{1,0},{2,3},{3,2},{4,5},{5,4},{6,7},{7,6},{8,9},{9,8},{10,11... | collective-permute-start | bytes 786440 | tf_op jit(solution)/shard_map/ppermute | solution.py:296
  15.2 0.0 copy-done
  15.3 0.0 copy-done.1
  15.3 0.0 copy-done.4
  15.3 0.6 fusion
  15.9 0.5 collective-permute-done
  16.4 13.2 %all_to_all.20 = f32[32,8,256]{2,1,0:T(8,128)S(1)} all-to-all(f32[32,8,256]{2,1,0:T(8,128)S(1)} %add_bitcast_fusion), channel_id=1, replica_groups=mesh['z'=12,'x'=4,'y'=8,'core'=2] {'x','y'}, dimensions={0} | all-to-all | bytes 524288 | tf_op jit(solution)/shard_map/all_to_all | solution.py:275
  29.7 16.0 %all_to_all.21 = f32[32,8,256]{2,1,0:T(8,128)S(1)} all-to-all(f32[32,8,256]{2,1,0:T(8,128)S(1)} %broadcast_in_dim.2), channel_id=1, replica_groups=mesh['z'=12,'x'=4,'y'=8,'core'=2] {'x','y'}, dimensions={0} | all-to-all | bytes 524288 | tf_op jit(solution)/shard_map/all_to_all | solution.py:275
  45.6 5.4 %all_gather.12.left_ref = f32[512,256]{1,0:T(8,128)S(1)} all-gather(f32[256,256]{1,0:T(8,128)S(1)} %bitcast.8), channel_id=1, replica_groups=mesh['z'=12,'x'=4,'y'=8,'core'=2] {'core'}, dimensions={0}, use_global_device_ids=true | all-gather | bytes 786432 | tf_op jit(solution)/shard_map/all_gather | solution.py:301
  51.0 1.5 %shard_map.68 = f32[12,104,128]{2,1,0:T(8,128)S(1)} custom-call(s32[1]{0:T(128)} %bitcast.core_ref, f32[512,512]{1,0:T(8,128)S(1)} %copy-done, bf16[512,512]{1,0:T(8,128)(2,1)S(1)} %copy-done.1, f32[512,256]{1,0:T(8,128)S(1)} %all_gather.12.left_ref), custom_call_target="tpu_custom_call" | custom-call | flops 1000000000 | bytes 4194304 | tf_op jit(solution)/shard_map/pallas_call | solution.py:306
  52.6 38.2 %all_to_all.22 = f32[12,104,128]{2,1,0:T(8,128)S(1)} all-to-all(f32[12,104,128]{2,1,0:T(8,128)S(1)} %shard_map.68), channel_id=1, replica_groups=mesh['z'=12,'x'=4,'y'=8,'core'=2] {'z'}, dimensions={0} | all-to-all | bytes 1277952 | tf_op jit(solution)/shard_map/all_to_all | solution.py:275
  90.8 4.4 %all_gather.13 = f32[32,128]{1,0:T(8,128)S(1)} all-gather(f32[16,128]{1,0:T(8,128)S(1)} %slice.9), channel_id=1, replica_groups=mesh['z'=12,'x'=4,'y'=8,'core'=2] {'core'}, dimensions={0}, use_global_device_ids=true | all-gather | bytes 24576 | tf_op jit(solution)/shard_map/all_gather | solution.py:313
  95.2 20.4 %all-gather = f32[1440,128]{1,0:T(8,128)S(1)} all-gather(f32[120,128]{1,0:T(8,128)S(1)} %pad_maximum_fusion), channel_id=2, replica_groups=mesh['z'=12,'x'=4,'y'=8,'core'=2] {'z'}, dimensions={0}, use_global_device_ids=true | all-gather | bytes 798720 | tf_op jit(solution)/shard_map/all_gather | solution.py:314
  115.6 9.1 %shard_map.69 = (f32[256,256]{1,0:T(8,128)S(1)}, f32[512,256]{1,0:T(8,128)S(1)}, f32[64,1,256]{2,1,0:T(1,128)}) custom-call(f32[12,120,128]{2,1,0:T(8,128)S(1)} %bitcast.7), custom_call_target="tpu_custom_call" | custom-call | flops 10000000000 | bytes 33554432 | tf_op jit(solution)/shard_map/pallas_call | solution.py:316
  124.7 0.0 copy-start.2
  124.7 10.1 %all-to-all-start.3 = ((f32[64,1,256]{2,1,0:T(1,128)}), f32[64,1,256]{2,1,0:T(1,128)S(1)}, u32[]{:S(2)}, u32[]{:S(2)}) async-start(f32[64,1,256]{2,1,0:T(1,128)} %get-tuple-element.14), calls=%async_computation.3 | async-start | bytes 131072 | tf_op jit(solution)/shard_map/all_to_all | solution.py:275
  134.7 2.8 %shard_map.70 = (f32[512,512]{1,0:T(8,128)}, f32[512,256]{1,0:T(8,128)S(1)}) custom-call(f32[256,256]{1,0:T(8,128)S(1)} %get-tuple-element.15.inv_ref, f32[512,256]{1,0:T(8,128)S(1)} %all_gather.12.left_ref, f32[512,256]{1,0:T(8,128)S(1)} %get-tuple-element.16.right_ref.refs_3_, f32[512,512]{1,0:T(8,128)S(1)} %copy-done, bf16[512,512]{1,0:T(8,128)(2,1)S(1)} %copy-done.1), custom_call_target="tpu_custom_call" | custom-call | flops 1000000000 | bytes 16777216 | tf_op jit(solution)/shard_map/pallas_call | solution.py:323
  137.5 0.0 copy-done.2
  137.5 0.0 copy-start.3
  137.5 0.8 copy-done.3
  138.3 6.2 %all-to-all-done.3.refs_0_ = f32[64,1,256]{2,1,0:T(1,128)S(1)} async-done(((f32[64,1,256]{2,1,0:T(1,128)}), f32[64,1,256]{2,1,0:T(1,128)S(1)}, u32[]{:S(2)}, u32[]{:S(2)}) %all-to-all-start.3) | async-done | bytes 65568 | tf_op jit(solution)/shard_map/all_to_all | solution.py:275
  144.5 3.0 %shard_map.71 = (f32[512,512]{1,0:T(8,128)}, f32[512,256]{1,0:T(8,128)}) custom-call(f32[64,1,256]{2,1,0:T(1,128)S(1)} %all-to-all-done.3.refs_0_, f32[512,512]{1,0:T(8,128)} %refs_1_.1, f32[512,256]{1,0:T(8,128)} %copy-done.3, f32[512,256]{1,0:T(8,128)} %copy-done.2), custom_call_target="tpu_custom_call" | custom-call | flops 1000000000 | bytes 4194304 | tf_op jit(solution)/shard_map/pallas_call | solution.py:257
  (7 shorter events, 0.1 us)
Async XLA Ops:
  0.6 14.6 %copy-start = (f32[512,512]{1,0:T(8,128)S(1)}, f32[512,512]{1,0:T(8,128)}, u32[]{:S(2)}) copy-start(f32[512,512]{1,0:T(8,128)} %momentum_ref.5) | copy-start | bytes 3145732
  0.6 14.6 %copy-start.1 = (bf16[512,512]{1,0:T(8,128)(2,1)S(1)}, bf16[512,512]{1,0:T(8,128)(2,1)}, u32[]{:S(2)}) copy-start(bf16[512,512]{1,0:T(8,128)(2,1)} %gradient_ref.5) | copy-start | bytes 1572868
  0.7 14.6 %copy-start.4 = (f32[512,256]{1,0:T(8,128)S(1)}, f32[512,256]{1,0:T(8,128)}, u32[]{:S(2)}) copy-start(f32[512,256]{1,0:T(8,128)} %right_ref.1) | copy-start | bytes 1572868
  2.8 13.6 %collective-permute-start = (f32[256,256]{1,0:T(8,128)S(1)}, f32[256,256]{1,0:T(8,128)S(1)}, u32[]{:S(2)}, u32[]{:S(2)}) collective-permute-start(f32[256,256]{1,0:T(8,128)S(1)} %shard_map.67), channel_id=1, source_target_pairs={{0,1},{1,0},{2,3},{3,2},{4,5},{5,4},{6,7},{7,6},{8,9},{9,8},{10,11... | collective-permute-start | bytes 786440 | tf_op jit(solution)/shard_map/ppermute | solution.py:296
  124.7 12.9 %copy-start.2 = (f32[512,256]{1,0:T(8,128)}, f32[512,256]{1,0:T(8,128)S(1)}, u32[]{:S(2)}) copy-start(f32[512,256]{1,0:T(8,128)S(1)} %get-tuple-element.16.right_ref.refs_3_) | copy-start | bytes 1572868
  124.7 19.9 %all-to-all-start.3 = ((f32[64,1,256]{2,1,0:T(1,128)}), f32[64,1,256]{2,1,0:T(1,128)S(1)}, u32[]{:S(2)}, u32[]{:S(2)}) async-start(f32[64,1,256]{2,1,0:T(1,128)} %get-tuple-element.14), calls=%async_computation.3 | async-start | bytes 131072 | tf_op jit(solution)/shard_map/all_to_all | solution.py:275
  137.5 0.8 copy-start.3

commit v8 on v7

--- a/solution.py
+++ b/solution.py
@@ -44,7 +44,7 @@
         for s in range(8):
             wide_ref[k % 2, 8 * s : 8 * s + 8, :] = cols[s]
         unit = jnp.where(own, jnp.where(lane == first + sub, 1.0, 0.0), top)
-        wide_ref[k % 2, 64:, :] = unit
+        wide_ref[k % 2, 64:72, :] = unit
         p = {(t, s): wide_ref[k % 2, pl.ds(8 * s + t, 8, stride=0), :] for s in range(8) for t in range(s, 8)}
         row = [wide_ref[k % 2, pl.ds(64 + s, 8, stride=0), :] for s in range(8)]
         low, inv = {}, []
@@ -312,7 +312,7 @@
     piece = exchange(pieces, "z").sum(0)
     shares = lax.all_gather(piece[top:], "core", axis=0, tiled=True)
     both = lax.all_gather(jnp.concatenate([piece[:top], shares], axis=0), "z")
-    scratch = [(2, half, half), (half, half), (2 * cols, half), (2, 72, half)]
+    scratch = [(2, half, half), (half, half), (2 * cols, half), (2, 80, half)]
     inverse, right_factor, sums = whole(
         functools.partial(right_kernel, top),
         (f32(rank, rank), f32(cols, rank), f32(2 * nxy, 1, rank)),

time: 148 us -> 148 us (level)
  no operation moved by 1% of the time
where the time goes in v8:
time: 148 us
  blocking collectives  97.5 us (66%)
  starting transfers between devices  22.5 us (15%)
  Pallas kernels  18.5 us (12%)
  waiting for transfers between devices  6.7 us (5%)
    all_to_all x3, blocking collectives, exchange(): return lax.all_to_all(blocks, axes, 0, 0)  67.3 us
    all_gather x1, blocking collectives, body(): both = lax.all_gather(jnp.concatenate([piece[:top], shares], axis=0), 'z')  20.4 us
    ppermute x1, starting transfers between devices, body(): lax.ppermute(other, 'core', [(0, 1), (1, 0)])  12.4 us
    all_to_all x1, starting transfers between devices, exchange(): return lax.all_to_all(blocks, axes, 0, 0)  10.1 us
    pallas_call x1, Pallas kernels, body(): whole(functools.partial(right_kernel, top), (f32(rank, rank), f32(cols, r...  9.08 us
    all_to_all x1, waiting for transfers between devices, exchange(): return lax.all_to_all(blocks, axes, 0, 0)  6.23 us
    all_gather x1, blocking collectives, body(): left_factor = lax.all_gather(half, 'core', axis=0, tiled=True)  5.41 us
    all_gather x1, blocking collectives, body(): shares = lax.all_gather(piece[top:], 'core', axis=0, tiled=True)  4.39 us
  transfers between devices with their start and end apart: 2, of which 2 were waited for; matrix products, arithmetic and copies ran while one was open for 0% of the time, Pallas kernels for 2%

profile of v8, /device:TPU:1, one launch (start us, length us, event | category | flops | bytes accessed | tf_op | source)
XLA Modules:
  0.0 147.5 jit_solution(12794332552600750392)
XLA Ops:
  0.6 0.0 copy-start
  0.6 0.0 copy-start.1
  0.7 0.0 copy-start.4
  0.7 2.1 %shard_map.67 = f32[256,256]{1,0:T(8,128)S(1)} custom-call(s32[1]{0:T(128)} %bitcast.1.half_ref, f32[512,512]{1,0:T(8,128)} %momentum_ref.5, bf16[512,512]{1,0:T(8,128)(2,1)} %gradient_ref.5, f32[512,256]{1,0:T(8,128)} %right_ref.1), custom_call_target="tpu_custom_call" | custom-call | flops 1000000000 | bytes 4194304 | tf_op jit(solution)/shard_map/pallas_call | solution.py:165
  2.8 12.4 %collective-permute-start = (f32[256,256]{1,0:T(8,128)S(1)}, f32[256,256]{1,0:T(8,128)S(1)}, u32[]{:S(2)}, u32[]{:S(2)}) collective-permute-start(f32[256,256]{1,0:T(8,128)S(1)} %shard_map.67), channel_id=1, source_target_pairs={{0,1},{1,0},{2,3},{3,2},{4,5},{5,4},{6,7},{7,6},{8,9},{9,8},{10,11... | collective-permute-start | bytes 786440 | tf_op jit(solution)/shard_map/ppermute | solution.py:296
  15.2 0.0 copy-done
  15.3 0.0 copy-done.1
  15.3 0.0 copy-done.4
  15.3 0.6 fusion
  15.9 0.5 collective-permute-done
  16.4 13.2 %all_to_all.20 = f32[32,8,256]{2,1,0:T(8,128)S(1)} all-to-all(f32[32,8,256]{2,1,0:T(8,128)S(1)} %add_bitcast_fusion), channel_id=1, replica_groups=mesh['z'=12,'x'=4,'y'=8,'core'=2] {'x','y'}, dimensions={0} | all-to-all | bytes 524288 | tf_op jit(solution)/shard_map/all_to_all | solution.py:275
  29.7 16.0 %all_to_all.21 = f32[32,8,256]{2,1,0:T(8,128)S(1)} all-to-all(f32[32,8,256]{2,1,0:T(8,128)S(1)} %broadcast_in_dim.2), channel_id=1, replica_groups=mesh['z'=12,'x'=4,'y'=8,'core'=2] {'x','y'}, dimensions={0} | all-to-all | bytes 524288 | tf_op jit(solution)/shard_map/all_to_all | solution.py:275
  45.6 5.4 %all_gather.12.left_ref = f32[512,256]{1,0:T(8,128)S(1)} all-gather(f32[256,256]{1,0:T(8,128)S(1)} %bitcast.8), channel_id=1, replica_groups=mesh['z'=12,'x'=4,'y'=8,'core'=2] {'core'}, dimensions={0}, use_global_device_ids=true | all-gather | bytes 786432 | tf_op jit(solution)/shard_map/all_gather | solution.py:301
  51.0 1.5 %shard_map.68 = f32[12,104,128]{2,1,0:T(8,128)S(1)} custom-call(s32[1]{0:T(128)} %bitcast.core_ref, f32[512,512]{1,0:T(8,128)S(1)} %copy-done, bf16[512,512]{1,0:T(8,128)(2,1)S(1)} %copy-done.1, f32[512,256]{1,0:T(8,128)S(1)} %all_gather.12.left_ref), custom_call_target="tpu_custom_call" | custom-call | flops 1000000000 | bytes 4194304 | tf_op jit(solution)/shard_map/pallas_call | solution.py:306
  52.6 38.2 %all_to_all.22 = f32[12,104,128]{2,1,0:T(8,128)S(1)} all-to-all(f32[12,104,128]{2,1,0:T(8,128)S(1)} %shard_map.68), channel_id=1, replica_groups=mesh['z'=12,'x'=4,'y'=8,'core'=2] {'z'}, dimensions={0} | all-to-all | bytes 1277952 | tf_op jit(solution)/shard_map/all_to_all | solution.py:275
  90.8 4.4 %all_gather.13 = f32[32,128]{1,0:T(8,128)S(1)} all-gather(f32[16,128]{1,0:T(8,128)S(1)} %slice.9), channel_id=1, replica_groups=mesh['z'=12,'x'=4,'y'=8,'core'=2] {'core'}, dimensions={0}, use_global_device_ids=true | all-gather | bytes 24576 | tf_op jit(solution)/shard_map/all_gather | solution.py:313
  95.2 20.4 %all-gather = f32[1440,128]{1,0:T(8,128)S(1)} all-gather(f32[120,128]{1,0:T(8,128)S(1)} %pad_maximum_fusion), channel_id=2, replica_groups=mesh['z'=12,'x'=4,'y'=8,'core'=2] {'z'}, dimensions={0}, use_global_device_ids=true | all-gather | bytes 798720 | tf_op jit(solution)/shard_map/all_gather | solution.py:314
  115.6 9.1 %shard_map.69 = (f32[256,256]{1,0:T(8,128)S(1)}, f32[512,256]{1,0:T(8,128)S(1)}, f32[64,1,256]{2,1,0:T(1,128)}) custom-call(f32[12,120,128]{2,1,0:T(8,128)S(1)} %bitcast.7), custom_call_target="tpu_custom_call" | custom-call | flops 10000000000 | bytes 33554432 | tf_op jit(solution)/shard_map/pallas_call | solution.py:316
  124.7 0.0 copy-start.2
  124.7 10.1 %all-to-all-start.3 = ((f32[64,1,256]{2,1,0:T(1,128)}), f32[64,1,256]{2,1,0:T(1,128)S(1)}, u32[]{:S(2)}, u32[]{:S(2)}) async-start(f32[64,1,256]{2,1,0:T(1,128)} %get-tuple-element.14), calls=%async_computation.3 | async-start | bytes 131072 | tf_op jit(solution)/shard_map/all_to_all | solution.py:275
  134.7 2.8 %shard_map.70 = (f32[512,512]{1,0:T(8,128)}, f32[512,256]{1,0:T(8,128)S(1)}) custom-call(f32[256,256]{1,0:T(8,128)S(1)} %get-tuple-element.15.inv_ref, f32[512,256]{1,0:T(8,128)S(1)} %all_gather.12.left_ref, f32[512,256]{1,0:T(8,128)S(1)} %get-tuple-element.16.right_ref.refs_3_, f32[512,512]{1,0:T(8,128)S(1)} %copy-done, bf16[512,512]{1,0:T(8,128)(2,1)S(1)} %copy-done.1), custom_call_target="tpu_custom_call" | custom-call | flops 1000000000 | bytes 16777216 | tf_op jit(solution)/shard_map/pallas_call | solution.py:323
  137.5 0.0 copy-done.2
  137.5 0.0 copy-start.3
  137.5 0.8 copy-done.3
  138.3 6.2 %all-to-all-done.3.refs_0_ = f32[64,1,256]{2,1,0:T(1,128)S(1)} async-done(((f32[64,1,256]{2,1,0:T(1,128)}), f32[64,1,256]{2,1,0:T(1,128)S(1)}, u32[]{:S(2)}, u32[]{:S(2)}) %all-to-all-start.3) | async-done | bytes 65568 | tf_op jit(solution)/shard_map/all_to_all | solution.py:275
  144.5 3.0 %shard_map.71 = (f32[512,512]{1,0:T(8,128)}, f32[512,256]{1,0:T(8,128)}) custom-call(f32[64,1,256]{2,1,0:T(1,128)S(1)} %all-to-all-done.3.refs_0_, f32[512,512]{1,0:T(8,128)} %refs_1_.1, f32[512,256]{1,0:T(8,128)} %copy-done.3, f32[512,256]{1,0:T(8,128)} %copy-done.2), custom_call_target="tpu_custom_call" | custom-call | flops 1000000000 | bytes 4194304 | tf_op jit(solution)/shard_map/pallas_call | solution.py:257
  (7 shorter events, 0.1 us)
Async XLA Ops:
  0.6 14.6 %copy-start = (f32[512,512]{1,0:T(8,128)S(1)}, f32[512,512]{1,0:T(8,128)}, u32[]{:S(2)}) copy-start(f32[512,512]{1,0:T(8,128)} %momentum_ref.5) | copy-start | bytes 3145732
  0.6 14.6 %copy-start.1 = (bf16[512,512]{1,0:T(8,128)(2,1)S(1)}, bf16[512,512]{1,0:T(8,128)(2,1)}, u32[]{:S(2)}) copy-start(bf16[512,512]{1,0:T(8,128)(2,1)} %gradient_ref.5) | copy-start | bytes 1572868
  0.7 14.6 %copy-start.4 = (f32[512,256]{1,0:T(8,128)S(1)}, f32[512,256]{1,0:T(8,128)}, u32[]{:S(2)}) copy-start(f32[512,256]{1,0:T(8,128)} %right_ref.1) | copy-start | bytes 1572868
  2.8 13.6 %collective-permute-start = (f32[256,256]{1,0:T(8,128)S(1)}, f32[256,256]{1,0:T(8,128)S(1)}, u32[]{:S(2)}, u32[]{:S(2)}) collective-permute-start(f32[256,256]{1,0:T(8,128)S(1)} %shard_map.67), channel_id=1, source_target_pairs={{0,1},{1,0},{2,3},{3,2},{4,5},{5,4},{6,7},{7,6},{8,9},{9,8},{10,11... | collective-permute-start | bytes 786440 | tf_op jit(solution)/shard_map/ppermute | solution.py:296
  124.7 12.9 %copy-start.2 = (f32[512,256]{1,0:T(8,128)}, f32[512,256]{1,0:T(8,128)S(1)}, u32[]{:S(2)}) copy-start(f32[512,256]{1,0:T(8,128)S(1)} %get-tuple-element.16.right_ref.refs_3_) | copy-start | bytes 1572868
  124.7 19.9 %all-to-all-start.3 = ((f32[64,1,256]{2,1,0:T(1,128)}), f32[64,1,256]{2,1,0:T(1,128)S(1)}, u32[]{:S(2)}, u32[]{:S(2)}) async-start(f32[64,1,256]{2,1,0:T(1,128)} %get-tuple-element.14), calls=%async_computation.3 | async-start | bytes 131072 | tf_op jit(solution)/shard_map/all_to_all | solution.py:275
  137.5 0.8 copy-start.3
